TPU v7x, 1024 devices: a whole 4x8x16 slice. The times are simulated.
1024 devices in a mesh: group: 8 (over y), expert: 64 (over x, z), ffn: 2 (over core).
Axes of the slice: x: 4, y: 8, z: 16, core: 2. Of those that a mesh axis runs over, the one named last changes fastest.
Arguments:
- tokens: bfloat16 [2048, 3584], P(('group', 'expert')), may hold values from -6 to 6
- cotangent: bfloat16 [2048, 3584], P(('group', 'expert')), may hold values from -6 to 6
- group_ids: int32 [2048, 4], P(('group', 'expert')), may hold values from 0 to 7, as said below
- expert_ids: int32 [2048, 8], P(('group', 'expert')), may hold values from 0 to 15, as said below
- gate_weights: bfloat16 [2048, 8], P(('group', 'expert')), may hold values from 0.049804688 to 0.5
- w_gate: bfloat16 [512, 3584, 256], P(('group', 'expert'), None, 'ffn'), may hold values from -0.09375 to 0.09375
- w_up: bfloat16 [512, 3584, 256], P(('group', 'expert'), None, 'ffn'), may hold values from -0.09375 to 0.09375
- w_down: bfloat16 [512, 256, 3584], P(('group', 'expert'), 'ffn'), may hold values from -0.1875 to 0.1875
Outputs:
- mixed: bfloat16 [2048, 3584], P(('group', 'expert'), 'ffn')
- token_grad: bfloat16 [2048, 3584], P(('group', 'expert'), 'ffn')
- gate_grad: float32 [2048, 8], P(('group', 'expert'), 'ffn')
Inputs may be any that keep to these rules, and one draw needn't show every extreme that they name: `group_ids`: each row names 4 different groups. `expert_ids`: entries 2 j and 2 j + 1 of a row are two different experts of group group_ids[t, j].
All inputs are finite; a program needn't handle non-finite values.
Results may differ from a plain program's by a relative error of at most 0.025.
Values may be sent and summed in bfloat16 or wider, within the bound.
A program may use at most 32 MiB of HBM per device.

v0:
```python
import jax
import jax.numpy as jnp
from jax import lax
from jax.sharding import PartitionSpec as P

EXPERTS = 128
CAP = 2


def body(tokens, cotangent, group_ids, expert_ids, gate_weights, w_gate, w_up, w_down):
    ngroup = lax.axis_size("group")
    nexpert = lax.axis_size("expert")
    ffn_count = lax.axis_size("ffn")
    ffn_index = lax.axis_index("ffn")
    per_group = EXPERTS // ngroup
    local_count = w_gate.shape[0]
    sub_count = max(nexpert // per_group, 1)
    tok_count, row_width = tokens.shape
    half_width = row_width // ffn_count
    pick_count = expert_ids.shape[1]
    pair_count = pick_count // group_ids.shape[1]
    pick_group = jnp.repeat(group_ids, pair_count, axis=1)
    group_hot = (pick_group[:, :, None] == jnp.arange(ngroup)[None, None, :]).astype(jnp.float32)
    expert_hot = (expert_ids[:, :, None] == jnp.arange(per_group)[None, None, :]).astype(
        jnp.float32
    )
    routing = jnp.einsum(
        "ik,ikh,ikx->hix",
        gate_weights.astype(jnp.float32),
        group_hot,
        expert_hot,
        precision=lax.Precision.HIGHEST,
    ).astype(jnp.bfloat16)
    chosen_mask = (jnp.sum(group_hot, axis=1) > 0).T[:, :, None]
    zero_value = jnp.zeros((), jnp.bfloat16)
    row_buffer = jnp.where(chosen_mask, tokens[None], zero_value)
    grad_buffer = jnp.where(chosen_mask, cotangent[None], zero_value)
    got_rows, got_grads, got_routing = (
        lax.all_to_all(row_buffer, "group", split_axis=0, concat_axis=0, tiled=True),
        lax.all_to_all(grad_buffer, "group", split_axis=0, concat_axis=0, tiled=True),
        lax.all_to_all(routing, "group", split_axis=0, concat_axis=0, tiled=True),
    )
    block_rows = ngroup * tok_count
    columns = got_rows.shape[2]
    flat_rows = got_rows.reshape(block_rows, columns)
    flat_grads = got_grads.reshape(block_rows, columns)
    flat_route = got_routing.reshape(block_rows, per_group)
    picked = (flat_route > 0).astype(jnp.int32)
    before = jnp.cumsum(picked, axis=0) - picked
    slot_ids = jnp.arange(CAP)
    select = ((before[:, :, None] == slot_ids[None, None, :]) & (picked[:, :, None] > 0)).astype(
        jnp.bfloat16
    )
    packed_rows = jnp.einsum(
        "rxc,rd->xcd", select, flat_rows, preferred_element_type=jnp.float32
    ).astype(jnp.bfloat16)
    packed_grads = jnp.einsum(
        "rxc,rd->xcd", select, flat_grads, preferred_element_type=jnp.float32
    ).astype(jnp.bfloat16)
    outgoing_rows = jnp.repeat(packed_rows, sub_count, axis=0).reshape(
        nexpert, local_count, CAP, columns
    )
    outgoing_grads = jnp.repeat(packed_grads, sub_count, axis=0).reshape(
        nexpert, local_count, CAP, columns
    )
    rows_in = lax.all_to_all(outgoing_rows, "expert", split_axis=0, concat_axis=0, tiled=True)
    grads_in = lax.all_to_all(outgoing_grads, "expert", split_axis=0, concat_axis=0, tiled=True)
    gate_pre = jnp.einsum("slcd,ldh->slch", rows_in, w_gate, preferred_element_type=jnp.float32)
    up_pre = jnp.einsum("slcd,ldh->slch", rows_in, w_up, preferred_element_type=jnp.float32)
    sigmoid_gate = jax.nn.sigmoid(gate_pre)
    active = gate_pre * sigmoid_gate
    hidden = (active * up_pre).astype(jnp.bfloat16)
    outputs = jnp.einsum(
        "slch,lhd->slcd", hidden, w_down, preferred_element_type=jnp.float32
    ).astype(jnp.bfloat16)
    back_hidden = jnp.einsum("slcd,lhd->slch", grads_in, w_down, preferred_element_type=jnp.float32)
    gate_back = (
        back_hidden * up_pre * sigmoid_gate * (1.0 + gate_pre * (1.0 - sigmoid_gate))
    ).astype(jnp.bfloat16)
    up_back = (back_hidden * active).astype(jnp.bfloat16)
    input_back = (
        jnp.einsum("slch,ldh->slcd", gate_back, w_gate, preferred_element_type=jnp.float32)
        + jnp.einsum("slch,ldh->slcd", up_back, w_up, preferred_element_type=jnp.float32)
    ).astype(jnp.bfloat16)
    inner_score = jnp.einsum(
        "slcd,slcd->slc", grads_in, outputs, preferred_element_type=jnp.float32
    ).astype(jnp.bfloat16)
    returned_out = lax.all_to_all(outputs, "expert", split_axis=0, concat_axis=0, tiled=True)
    returned_in = lax.all_to_all(input_back, "expert", split_axis=0, concat_axis=0, tiled=True)
    returned_score = lax.all_to_all(inner_score, "expert", split_axis=0, concat_axis=0, tiled=True)
    back_out = returned_out.reshape(per_group, sub_count, CAP, ffn_count, half_width)
    back_in = returned_in.reshape(per_group, sub_count, CAP, ffn_count, half_width)
    back_score = returned_score.reshape(per_group, sub_count, CAP)
    weighted = (select * flat_route[:, :, None]).reshape(ngroup, tok_count, per_group, CAP)
    mixed_rows = jnp.einsum(
        "gixc,xscfh->gfih", weighted, back_out, preferred_element_type=jnp.float32
    )
    grad_rows = jnp.einsum(
        "gixc,xscfh->gfih", weighted, back_in, preferred_element_type=jnp.float32
    )
    mixed_rows = mixed_rows.reshape(ngroup * ffn_count, tok_count, half_width)
    grad_rows = grad_rows.reshape(ngroup * ffn_count, tok_count, half_width)
    score_rows = jnp.einsum("rxc,xsc->rx", select, back_score, preferred_element_type=jnp.float32)
    score_rows = jnp.broadcast_to(
        score_rows.reshape(ngroup, 1, tok_count, per_group),
        (ngroup, ffn_count, tok_count, per_group),
    ).reshape(ngroup * ffn_count, tok_count, per_group)
    got_mixed, got_grad, got_score = (
        lax.all_to_all(mixed_rows, ("group", "ffn"), split_axis=0, concat_axis=0, tiled=True),
        lax.all_to_all(grad_rows, ("group", "ffn"), split_axis=0, concat_axis=0, tiled=True),
        lax.all_to_all(score_rows, ("group", "ffn"), split_axis=0, concat_axis=0, tiled=True),
    )
    mixed = jnp.sum(got_mixed, axis=0).astype(jnp.bfloat16)
    token_grad = jnp.sum(got_grad, axis=0).astype(jnp.bfloat16)
    group_scores = jnp.sum(got_score.reshape(ngroup, ffn_count, tok_count, per_group), axis=1)
    all_scores = jnp.einsum(
        "hix,ikh,ikx->ik", group_scores, group_hot, expert_hot, precision=lax.Precision.HIGHEST
    )
    share = pick_count // ffn_count
    gate_grad = lax.dynamic_slice_in_dim(all_scores, ffn_index * share, share, 1)
    return (mixed, token_grad, gate_grad)


def solution(mesh):
    return jax.shard_map(
        body,
        mesh=mesh,
        in_specs=(
            P(("group", "expert"), None),
            P(("group", "expert"), None),
            P(("group", "expert"), None),
            P(("group", "expert"), None),
            P(("group", "expert"), None),
            P(("group", "expert"), None, "ffn"),
            P(("group", "expert"), None, "ffn"),
            P(("group", "expert"), "ffn", None),
        ),
        out_specs=(
            P(("group", "expert"), "ffn"),
            P(("group", "expert"), "ffn"),
            P(("group", "expert"), "ffn"),
        ),
        check_vma=False,
    )
```

profile of v0, /device:TPU:1, one launch (start us, length us, event | category | flops | bytes accessed | tf_op | source)
XLA Modules:
  0.0 350.3 jit_solution(6198487666220581060)
XLA Ops:
  0.6 0.8 copy.131
  1.6 0.7 convert.9
  2.3 0.9 fusion.4
  3.1 0.6 copy.133
  3.8 7.7 %all-to-all-start = ((bf16[8,4,16]{2,1,0:T(4,128)(2,1)}), bf16[8,4,16]{2,1,0:T(4,128)(2,1)S(1)}, u32[]{:S(2)}, u32[]{:S(2)}) async-start(bf16[8,4,16]{2,1,0:T(4,128)(2,1)} %copy.133), calls=%async_computation | async-start | bytes 16384 | tf_op jit(solution)/shard_map/all_to_all | solution.py:41
  11.6 1.8 broadcast_select_fusion
  13.4 4.6 %all-to-all-done = bf16[8,4,16]{2,1,0:T(4,128)(2,1)S(1)} async-done(((bf16[8,4,16]{2,1,0:T(4,128)(2,1)}), bf16[8,4,16]{2,1,0:T(4,128)(2,1)S(1)}, u32[]{:S(2)}, u32[]{:S(2)}) %all-to-all-start) | async-done | bytes 1056 | tf_op jit(solution)/shard_map/all_to_all | solution.py:41
  18.0 3.4 all-to-all-start.1
  21.8 1.9 fusion.57
  23.9 6.5 %all-to-all-done.1 = bf16[8,4,3584]{2,1,0:T(4,128)(2,1)S(1)} async-done(((bf16[8,4,3584]{2,1,0:T(4,128)(2,1)}), bf16[8,4,3584]{2,1,0:T(4,128)(2,1)S(1)}, u32[]{:S(2)}, u32[]{:S(2)}) %all-to-all-start.1) | async-done | bytes 229408 | tf_op jit(solution)/shard_map/all_to_all | solution.py:39
  30.4 3.4 all-to-all-start.5
  34.3 10.0 %all-to-all-done.5 = bf16[8,4,3584]{2,1,0:T(4,128)(2,1)S(1)} async-done(((bf16[8,4,3584]{2,1,0:T(4,128)(2,1)}), bf16[8,4,3584]{2,1,0:T(4,128)(2,1)S(1)}, u32[]{:S(2)}, u32[]{:S(2)}) %all-to-all-start.5) | async-done | bytes 229408 | tf_op jit(solution)/shard_map/all_to_all | solution.py:40
  44.3 1.4 broadcast_in_dim.58
  45.7 20.4 %all-to-all-start.2 = ((bf16[64,1,2,3584]{3,2,1,0:T(2,128)(2,1)}), bf16[64,1,2,3584]{3,2,1,0:T(2,128)(2,1)S(1)}, u32[]{:S(2)}, u32[]{:S(2)}) async-start(bf16[64,1,2,3584]{3,2,1,0:T(2,128)(2,1)} %bitcast.7), calls=%async_computation.2 | async-start | bytes 1835008 | tf_op jit(solution)/shard_map/all_to_all | solution.py:66
  66.6 41.2 %all-to-all-done.2 = bf16[64,1,2,3584]{3,2,1,0:T(2,128)(2,1)S(1)} async-done(((bf16[64,1,2,3584]{3,2,1,0:T(2,128)(2,1)}), bf16[64,1,2,3584]{3,2,1,0:T(2,128)(2,1)S(1)}, u32[]{:S(2)}, u32[]{:S(2)}) %all-to-all-start.2) | async-done | bytes 917536 | tf_op jit(solution)/shard_map/all_to_all | solution.py:66
  107.8 1.4 broadcast_in_dim.60
  109.2 10.3 %all-to-all-start.6 = ((bf16[64,1,2,3584]{3,2,1,0:T(2,128)(2,1)}), bf16[64,1,2,3584]{3,2,1,0:T(2,128)(2,1)S(1)}, u32[]{:S(2)}, u32[]{:S(2)}) async-start(bf16[64,1,2,3584]{3,2,1,0:T(2,128)(2,1)} %bitcast.33), calls=%async_computation.6 | async-start | bytes 1835008 | tf_op jit(solution)/shard_map/all_to_all | solution.py:67
  119.6 1.6 convolution_bitcast_fusion.4
  121.6 39.7 %all-to-all-done.6 = bf16[64,1,2,3584]{3,2,1,0:T(2,128)(2,1)S(1)} async-done(((bf16[64,1,2,3584]{3,2,1,0:T(2,128)(2,1)}), bf16[64,1,2,3584]{3,2,1,0:T(2,128)(2,1)S(1)}, u32[]{:S(2)}, u32[]{:S(2)}) %all-to-all-start.6) | async-done | bytes 917536 | tf_op jit(solution)/shard_map/all_to_all | solution.py:67
  161.3 0.5 fusion.2
  161.9 24.7 %all_to_all.55 = bf16[64,1,2]{2,1,0:T(2,128)(2,1)S(1)} all-to-all(bf16[64,1,2]{2,1,0:T(2,128)(2,1)S(1)} %copy.154), channel_id=1, replica_groups=mesh['group'=8,'expert'=64,'ffn'=2] {'expert'}, dimensions={0} | all-to-all | bytes 512 | tf_op jit(solution)/shard_map/all_to_all | solution.py:90
  187.0 0.6 broadcast_in_dim.62
  187.6 7.1 %all-to-all-start.10 = ((f32[16,4,16]{2,1,0:T(4,128)}), f32[16,4,16]{2,1,0:T(4,128)S(1)}, u32[]{:S(2)}, u32[]{:S(2)}) async-start(f32[16,4,16]{2,1,0:T(4,128)} %bitcast.55), calls=%async_computation.10 | async-start | bytes 65536 | tf_op jit(solution)/shard_map/all_to_all | solution.py:111
  194.8 1.9 copy.141
  196.7 5.6 %all-to-all-done.10 = f32[16,4,16]{2,1,0:T(4,128)S(1)} async-done(((f32[16,4,16]{2,1,0:T(4,128)}), f32[16,4,16]{2,1,0:T(4,128)S(1)}, u32[]{:S(2)}, u32[]{:S(2)}) %all-to-all-start.10) | async-done | bytes 4128 | tf_op jit(solution)/shard_map/all_to_all | solution.py:111
  202.2 4.6 %all-to-all-start.3 = ((bf16[64,1,2,3584]{3,2,1,0:T(2,128)(2,1)}), bf16[64,1,2,3584]{3,2,1,0:T(2,128)(2,1)S(1)}, u32[]{:S(2)}, u32[]{:S(2)}) async-start(bf16[64,1,2,3584]{3,2,1,0:T(2,128)(2,1)} %copy.141), calls=%async_computation.3 | async-start | bytes 1835008 | tf_op jit(solution)/shard_map/all_to_all | solution.py:88
  207.3 0.8 copy-done.2
  208.1 0.4 fusion.10
  208.5 0.8 copy-done.4
  209.3 0.4 fusion.1
  209.7 1.9 copy.150
  211.5 41.1 %all-to-all-done.3 = bf16[64,1,2,3584]{3,2,1,0:T(2,128)(2,1)S(1)} async-done(((bf16[64,1,2,3584]{3,2,1,0:T(2,128)(2,1)}), bf16[64,1,2,3584]{3,2,1,0:T(2,128)(2,1)S(1)}, u32[]{:S(2)}, u32[]{:S(2)}) %all-to-all-start.3) | async-done | bytes 917536 | tf_op jit(solution)/shard_map/all_to_all | solution.py:88
  252.7 9.6 %all-to-all-start.7 = ((bf16[64,1,2,3584]{3,2,1,0:T(2,128)(2,1)}), bf16[64,1,2,3584]{3,2,1,0:T(2,128)(2,1)}, u32[]{:S(2)}, u32[]{:S(2)}) async-start(bf16[64,1,2,3584]{3,2,1,0:T(2,128)(2,1)} %copy.150), calls=%async_computation.7 | async-start | bytes 1835008 | tf_op jit(solution)/shard_map/all_to_all | solution.py:89
  262.3 0.6 reduce.3
  262.9 3.2 reshape.140
  266.2 1.1 reduce_sum.64
  267.7 1.0 copy.147
  268.7 38.9 %all-to-all-done.7 = bf16[64,1,2,3584]{3,2,1,0:T(2,128)(2,1)} async-done(((bf16[64,1,2,3584]{3,2,1,0:T(2,128)(2,1)}), bf16[64,1,2,3584]{3,2,1,0:T(2,128)(2,1)}, u32[]{:S(2)}, u32[]{:S(2)}) %all-to-all-start.7) | async-done | bytes 917536 | tf_op jit(solution)/shard_map/all_to_all | solution.py:89
  307.6 7.3 %all-to-all-start.4 = ((f32[16,4,1792]{2,1,0:T(4,128)}), f32[16,4,1792]{2,1,0:T(4,128)S(1)}, u32[]{:S(2)}, u32[]{:S(2)}) async-start(f32[16,4,1792]{2,1,0:T(4,128)} %bitcast.32), calls=%async_computation.4 | async-start | bytes 917504 | tf_op jit(solution)/shard_map/all_to_all | solution.py:109
  314.9 3.2 reshape.141
  318.1 1.1 reduce_sum.66
  319.6 0.9 copy.153
  320.6 10.3 %all-to-all-done.4 = f32[16,4,1792]{2,1,0:T(4,128)S(1)} async-done(((f32[16,4,1792]{2,1,0:T(4,128)}), f32[16,4,1792]{2,1,0:T(4,128)S(1)}, u32[]{:S(2)}, u32[]{:S(2)}) %all-to-all-start.4) | async-done | bytes 458784 | tf_op jit(solution)/shard_map/all_to_all | solution.py:109
  330.8 3.5 all-to-all-start.8
  334.7 0.7 constant_dynamic-slice_fusion
  335.4 0.7 reduce_sum.65
  336.0 13.6 %all-to-all-done.8 = f32[16,4,1792]{2,1,0:T(4,128)S(1)} async-done(((f32[16,4,1792]{2,1,0:T(4,128)}), f32[16,4,1792]{2,1,0:T(4,128)S(1)}, u32[]{:S(2)}, u32[]{:S(2)}) %all-to-all-start.8) | async-done | bytes 458784 | tf_op jit(solution)/shard_map/all_to_all | solution.py:110
  349.6 0.7 reduce_sum.67
  (48 shorter events, 4.5 us)
Async XLA Ops:
  0.6 160.7 %copy-start = (bf16[1,128,3584]{2,1,0:T(8,128)(2,1)S(1)}, bf16[1,128,3584]{2,1,0:T(8,128)(2,1)}, u32[]{:S(2)}) copy-start(bf16[1,128,3584]{2,1,0:T(8,128)(2,1)} %param.15) | copy-start | bytes 2752516
  3.8 14.2 %all-to-all-start = ((bf16[8,4,16]{2,1,0:T(4,128)(2,1)}), bf16[8,4,16]{2,1,0:T(4,128)(2,1)S(1)}, u32[]{:S(2)}, u32[]{:S(2)}) async-start(bf16[8,4,16]{2,1,0:T(4,128)(2,1)} %copy.133), calls=%async_computation | async-start | bytes 16384 | tf_op jit(solution)/shard_map/all_to_all | solution.py:41
  18.0 12.4 %all-to-all-start.1 = ((bf16[8,4,3584]{2,1,0:T(4,128)(2,1)}), bf16[8,4,3584]{2,1,0:T(4,128)(2,1)S(1)}, u32[]{:S(2)}, u32[]{:S(2)}) async-start(bf16[8,4,3584]{2,1,0:T(4,128)(2,1)} %get-tuple-element.6), calls=%async_computation.1 | async-start | bytes 458752 | tf_op jit(solution)/shard_map/all_to_all | solution.py:39
  30.4 13.9 %all-to-all-start.5 = ((bf16[8,4,3584]{2,1,0:T(4,128)(2,1)}), bf16[8,4,3584]{2,1,0:T(4,128)(2,1)S(1)}, u32[]{:S(2)}, u32[]{:S(2)}) async-start(bf16[8,4,3584]{2,1,0:T(4,128)(2,1)} %get-tuple-element.5), calls=%async_computation.5 | async-start | bytes 458752 | tf_op jit(solution)/shard_map/all_to_all | solution.py:40
  45.7 62.1 %all-to-all-start.2 = ((bf16[64,1,2,3584]{3,2,1,0:T(2,128)(2,1)}), bf16[64,1,2,3584]{3,2,1,0:T(2,128)(2,1)S(1)}, u32[]{:S(2)}, u32[]{:S(2)}) async-start(bf16[64,1,2,3584]{3,2,1,0:T(2,128)(2,1)} %bitcast.7), calls=%async_computation.2 | async-start | bytes 1835008 | tf_op jit(solution)/shard_map/all_to_all | solution.py:66
  109.2 52.1 %all-to-all-start.6 = ((bf16[64,1,2,3584]{3,2,1,0:T(2,128)(2,1)}), bf16[64,1,2,3584]{3,2,1,0:T(2,128)(2,1)S(1)}, u32[]{:S(2)}, u32[]{:S(2)}) async-start(bf16[64,1,2,3584]{3,2,1,0:T(2,128)(2,1)} %bitcast.33), calls=%async_computation.6 | async-start | bytes 1835008 | tf_op jit(solution)/shard_map/all_to_all | solution.py:67
  119.5 1.7 copy-start.3
  187.6 14.6 %all-to-all-start.10 = ((f32[16,4,16]{2,1,0:T(4,128)}), f32[16,4,16]{2,1,0:T(4,128)S(1)}, u32[]{:S(2)}, u32[]{:S(2)}) async-start(f32[16,4,16]{2,1,0:T(4,128)} %bitcast.55), calls=%async_computation.10 | async-start | bytes 65536 | tf_op jit(solution)/shard_map/all_to_all | solution.py:111
  202.2 50.4 %all-to-all-start.3 = ((bf16[64,1,2,3584]{3,2,1,0:T(2,128)(2,1)}), bf16[64,1,2,3584]{3,2,1,0:T(2,128)(2,1)S(1)}, u32[]{:S(2)}, u32[]{:S(2)}) async-start(bf16[64,1,2,3584]{3,2,1,0:T(2,128)(2,1)} %copy.141), calls=%async_computation.3 | async-start | bytes 1835008 | tf_op jit(solution)/shard_map/all_to_all | solution.py:88
  206.9 1.2 copy-start.2
  208.1 1.2 copy-start.4
  252.7 10.2 %copy-start.1 = (bf16[64,1,2,3584]{3,2,1,0:T(2,128)(2,1)}, bf16[64,1,2,3584]{3,2,1,0:T(2,128)(2,1)S(1)}, u32[]{:S(2)}) copy-start(bf16[64,1,2,3584]{3,2,1,0:T(2,128)(2,1)S(1)} %all-to-all-done.3) | copy-start | bytes 2752516
  252.7 54.9 %all-to-all-start.7 = ((bf16[64,1,2,3584]{3,2,1,0:T(2,128)(2,1)}), bf16[64,1,2,3584]{3,2,1,0:T(2,128)(2,1)}, u32[]{:S(2)}, u32[]{:S(2)}) async-start(bf16[64,1,2,3584]{3,2,1,0:T(2,128)(2,1)} %copy.150), calls=%async_computation.7 | async-start | bytes 1835008 | tf_op jit(solution)/shard_map/all_to_all | solution.py:89
  307.6 23.3 %all-to-all-start.4 = ((f32[16,4,1792]{2,1,0:T(4,128)}), f32[16,4,1792]{2,1,0:T(4,128)S(1)}, u32[]{:S(2)}, u32[]{:S(2)}) async-start(f32[16,4,1792]{2,1,0:T(4,128)} %bitcast.32), calls=%async_computation.4 | async-start | bytes 917504 | tf_op jit(solution)/shard_map/all_to_all | solution.py:109
  319.2 15.2 %copy-start.5 = (s32[4,8]{1,0:T(4,128)S(1)}, s32[4,8]{1,0:T(4,128)}, u32[]{:S(2)}) copy-start(s32[4,8]{1,0:T(4,128)} %param.11) | copy-start | bytes 388
  330.8 18.8 %all-to-all-start.8 = ((f32[16,4,1792]{2,1,0:T(4,128)}), f32[16,4,1792]{2,1,0:T(4,128)S(1)}, u32[]{:S(2)}, u32[]{:S(2)}) async-start(f32[16,4,1792]{2,1,0:T(4,128)} %bitcast.51), calls=%async_computation.8 | async-start | bytes 917504 | tf_op jit(solution)/shard_map/all_to_all | solution.py:110
where the time goes:
time: 352 us; the launch traced here: 350 us
  waiting for transfers between devices  211 us (60%)
  starting transfers between devices  77.3 us (22%)
  blocking collectives  24.7 us (7%)
  local copies, waits for them, and re-layouts  21.4 us (6%)
  other arithmetic  8.84 us (3%)
  matrix products  5.77 us (2%)
    all_to_all x1, waiting for transfers between devices, body(): lax.all_to_all(outgoing_rows, 'expert', split_axis=0, concat_axis=0, tile...  41.2 us
    all_to_all x1, waiting for transfers between devices, body(): lax.all_to_all(outputs, 'expert', split_axis=0, concat_axis=0, tiled=True)  41.1 us
    all_to_all x1, waiting for transfers between devices, body(): lax.all_to_all(outgoing_grads, 'expert', split_axis=0, concat_axis=0, til...  39.7 us
    all_to_all x1, waiting for transfers between devices, body(): lax.all_to_all(input_back, 'expert', split_axis=0, concat_axis=0, tiled=T...  38.9 us
    all_to_all x1, blocking collectives, body(): lax.all_to_all(inner_score, 'expert', split_axis=0, concat_axis=0, tiled=...  24.7 us
    all_to_all x1, starting transfers between devices, body(): lax.all_to_all(outgoing_rows, 'expert', split_axis=0, concat_axis=0, tile...  20.4 us
    all_to_all x1, waiting for transfers between devices, body(): lax.all_to_all(grad_rows, ('group', 'ffn'), split_axis=0, concat_axis=0,...  13.6 us
    all_to_all x1, starting transfers between devices, body(): lax.all_to_all(outgoing_grads, 'expert', split_axis=0, concat_axis=0, til...  10.3 us
  transfers between devices with their start and end apart: 10, of which 10 were waited for; matrix products, arithmetic and copies ran while one was open for 7% of the time, Pallas kernels for 0%

commit v1 on v0

v1 whole, which is shorter than its diff:
```python
import functools

import jax
import jax.numpy as jnp
from jax import lax
from jax.experimental import pallas as pl
from jax.experimental.pallas import tpu as pltpu
from jax.sharding import PartitionSpec as P

CAP = 2
NZ = 16
MESH = pl.DeviceIdType.MESH
F32 = jnp.float32
BF16 = jnp.bfloat16


def iota(shape, dim):
    return lax.broadcasted_iota(jnp.int32, shape, dim)


def dot(a, b):
    return jnp.dot(a, b, preferred_element_type=F32)


def dot_nt(a, b):
    return lax.dot_general(a, b, (((1,), (1,)), ((), ())), preferred_element_type=F32)


def kernel(
    ny, nx, per_group,
    tok_ref, cot_ref, gid_ref, eid_ref, gw_ref, wg_hbm, wu_hbm, wd_hbm,
    mixed_ref, grad_ref, score_ref,
    wg, wu, wd, wdt, wgt, wut,
    msg32, gbuf, ibuf, packed, xbuf, mbuf, zbuf, obuf, pin, cbuf, in_left, in_right,
    fin, rp, ret, ymsg, ybuf, smsg, sbuf,
    wsem, gs, gr, isem, ir, xs, xr, zds, zr, zfr, zfl, cs, cr, ps, pr,
    los, lor, ros, ror, fs, fr, xbs, xbr, ys, yr, ss, sr,
):
    y = lax.axis_index("group")
    e = lax.axis_index("expert")
    c = lax.axis_index("ffn")
    x = e // NZ
    z = e % NZ
    q = z // 4
    r = z % 4
    other = 1 - c
    width = msg32.shape[1]
    top_k = eid_ref.shape[1]
    rows_m = mbuf.shape[1]
    half_m = rows_m // 2
    quart_m = rows_m // 4
    n_in = ny * 16
    n_out = nx * 32

    def dev(yy, xx, zz, cc):
        return (yy, xx * NZ + zz, cc)

    def remote(src, dst, send, recv, where):
        return pltpu.make_async_remote_copy(
            src_ref=src, dst_ref=dst, send_sem=send, recv_sem=recv,
            device_id=where, device_id_type=MESH,
        )

    weight_copies = [
        pltpu.make_async_copy(wg_hbm.at[0], wg, wsem.at[0]),
        pltpu.make_async_copy(wu_hbm.at[0], wu, wsem.at[1]),
        pltpu.make_async_copy(wd_hbm.at[0], wd, wsem.at[2]),
    ]
    for cp in weight_copies:
        cp.start()

    barrier = pltpu.get_barrier_semaphore()
    partners = [dev(y, x, z, other)]
    for d in range(1, ny):
        for cc in range(2):
            partners.append(dev((y + d) % ny, x, z, cc))
    for d in range(1, nx):
        partners.append(dev(y, (x + d) % nx, z, c))
    for d in range(1, NZ):
        partners.append(dev(y, x, (z + d) % NZ, c))
    for where in partners:
        pl.semaphore_signal(barrier, inc=1, device_id=where, device_id_type=MESH)

    for h in range(2):
        for a, ref in enumerate((tok_ref, cot_ref)):
            start = pl.multiple_of(c * (2 * width) + h * width, 128)
            msg32[h * 8 + a * 4:h * 8 + a * 4 + 4, :] = ref[:, pl.ds(start, width)].astype(F32)
    gbuf[y] = msg32[...].astype(BF16)
    lane4 = iota((4, 128), 1)
    gid = gid_ref[...].astype(F32)
    eid = eid_ref[...].astype(F32)
    gw = gw_ref[...].astype(F32)
    info = jnp.zeros((4, 128), F32)
    for k in range(top_k):
        ident = gid[:, k // 2:k // 2 + 1] * float(per_group) + eid[:, k:k + 1]
        info = jnp.where(lane4 == k, ident, info)
        info = jnp.where(lane4 == top_k + k, gw[:, k:k + 1], info)
    ibuf[y] = jnp.full((8, 128), -1.0, F32)
    ibuf[y, 0:4, :] = info

    pl.semaphore_wait(barrier, len(partners))

    sends = []
    for d in range(1, ny):
        where = dev((y + d) % ny, x, z, c)
        sends.append(remote(ibuf.at[y], ibuf.at[y], isem.at[d], ir.at[d], where))
        sends[-1].start()
    for d in range(1, ny):
        where = dev((y + d) % ny, x, z, c)
        sends.append(remote(gbuf.at[y], gbuf.at[y], gs.at[d], gr.at[d], where))
        sends[-1].start()

    for cp in weight_copies:
        cp.wait()
    for k0 in range(0, wg.shape[0], 128):
        wgt[:, k0:k0 + 128] = wg[k0:k0 + 128, :].T
        wut[:, k0:k0 + 128] = wu[k0:k0 + 128, :].T
        wdt[k0:k0 + 128, :] = wd[:, k0:k0 + 128].T

    for d in range(1, ny):
        src = (y + ny - d) % ny
        remote(ibuf.at[src], ibuf.at[src], isem.at[d], ir.at[d], dev(src, x, z, c)).wait_recv()

    row_e = iota((n_in, ny * 8), 0)
    col_e = iota((n_in, ny * 8), 1)
    expand = ((row_e // 16 == col_e // 8) & (row_e % 4 == col_e % 8)).astype(F32).astype(BF16)
    known = dot(expand, ibuf[...].reshape(ny * 8, 128).astype(BF16))
    ri = iota((n_in, n_out), 0)
    lo = iota((n_in, n_out), 1)
    expert_o = (lo // 32) * 4 + (lo // 4) % 4
    target = (y * per_group + expert_o).astype(F32)
    slot_o = (lo % 2).astype(F32)
    same = ((ri // 4) % 2 == (lo // 2) % 2) & ((ri // 8) % 2 == (lo // 16) % 2)
    picked = jnp.zeros((n_in, n_out), F32)
    weight = jnp.zeros((n_in, n_out), F32)
    for k in range(top_k):
        hit = known[:, k:k + 1] == target
        picked = jnp.where(hit, 1.0, picked)
        weight = jnp.where(hit, known[:, top_k + k:top_k + k + 1], weight)
    rb = iota((n_in, n_in), 0)
    cb = iota((n_in, n_in), 1)
    earlier = (((cb // 16) * 4 + cb % 4) < ((rb // 16) * 4 + rb % 4)) & ((cb // 4) % 4 == 0)
    before = dot(earlier.astype(F32).astype(BF16), picked.astype(BF16))
    select = jnp.where((before == slot_o) & (picked > 0.0), 1.0, 0.0)
    pick_t = jnp.where(same, select, 0.0)
    pick_matrix = pick_t.T.astype(BF16)
    weight_matrix = (pick_t * weight).astype(BF16)

    for d in range(1, ny):
        src = (y + ny - d) % ny
        remote(gbuf.at[src], gbuf.at[src], gs.at[d], gr.at[d], dev(src, x, z, c)).wait_recv()
    packed[...] = dot(pick_matrix, gbuf[...].reshape(n_in, width)).astype(BF16).reshape(nx, 32, width)

    for d in range(1, nx):
        to = (x + d) % nx
        sends.append(remote(packed.at[to], xbuf.at[x], xs.at[d], xr.at[d], dev(y, to, z, c)))
        sends[-1].start()
    xbuf[x] = packed[x]
    for d in range(1, nx):
        src = (x + nx - d) % nx
        remote(packed.at[src], xbuf.at[src], xs.at[d], xr.at[d], dev(y, src, z, c)).wait_recv()
    rm = iota((n_out, n_out), 0)
    cm = iota((n_out, n_out), 1)

    def x_row(m):
        return ((m // 2) % nx) * 32 + ((m // half_m) % 2) * 16 + (m // rows_m) * 4 + ((m // quart_m) % 2) * 2 + m % 2

    to_quad = (cm == x_row(rm)).astype(F32).astype(BF16)
    from_quad = (rm == x_row(cm)).astype(F32).astype(BF16)
    mbuf[...] = dot(to_quad, xbuf[...].reshape(n_out, width)).astype(BF16).reshape(4, rows_m, width)

    zbuf[c, 6 + r] = mbuf[q]
    q1 = (q + 1) % 4
    q2 = (q + 2) % 4
    q3 = (q + 3) % 4
    end2 = jnp.where(r >= 2, 0, 3)
    id2 = (r + 14) % 16
    direct = [
        remote(mbuf.at[q2], zbuf.at[c, id2], zds.at[0], zr.at[id2], dev(y, x, 4 * q2 + end2, c)),
        remote(mbuf.at[q1], zbuf.at[c, r + 2], zds.at[1], zr.at[r + 2], dev(y, x, 4 * q1, c)),
        remote(mbuf.at[q3], zbuf.at[c, r + 10], zds.at[2], zr.at[r + 10], dev(y, x, 4 * q3 + 3, c)),
    ]
    z_right = (z + 1) % NZ
    z_left = (z + NZ - 1) % NZ

    def to_right(i):
        return remote(zbuf.at[c, i], zbuf.at[c, i], zfr.at[i], zr.at[i], dev(y, x, z_right, c))

    def to_left(i):
        return remote(zbuf.at[c, i], zbuf.at[c, i], zfl.at[i], zr.at[i], dev(y, x, z_left, c))

    def to_core(i):
        return remote(zbuf.at[c, i], zbuf.at[c, i], cs.at[i], cr.at[i], dev(y, x, z, other))

    def arrived(i):
        to_right(i).wait_recv()

    own = 6 + r
    for cp in direct:
        cp.start()
    sends += direct

    @pl.when(r < 3)
    def _():
        to_right(own).start()

    @pl.when(r > 0)
    def _():
        to_left(own).start()

    to_core(own).start()
    for k in range(1, 4):
        @pl.when(r >= k)
        def _():
            arrived(6 + r - k)

            @pl.when(r < 3)
            def _():
                to_right(6 + r - k).start()

            to_core(6 + r - k).start()

        @pl.when(r + k < 4)
        def _():
            arrived(6 + r + k)

            @pl.when(r > 0)
            def _():
                to_left(6 + r + k).start()

            to_core(6 + r + k).start()

    for j in range(6):
        right_id, left_id = 5 - j, 10 + j
        arrived(right_id)

        @pl.when(r < 3)
        def _():
            to_right(right_id).start()

        to_core(right_id).start()
        arrived(left_id)

        @pl.when(r > 0)
        def _():
            to_left(left_id).start()

        to_core(left_id).start()

    for i in range(16):
        remote(zbuf.at[other, i], zbuf.at[other, i], cs.at[i], cr.at[i], dev(y, x, z, other)).wait_recv()

    gate = up = back = None
    for cc in range(2):
        for h in range(2):
            rows = zbuf[cc, :, h * half_m:(h + 1) * half_m, :].reshape(16 * half_m, width)
            k0 = (2 * cc + h) * width
            parts = [dot(rows, w[k0:k0 + width, :]) for w in (wg, wu, wdt)]
            if gate is None:
                gate, up, back = parts
            else:
                gate, up, back = gate + parts[0], up + parts[1], back + parts[2]
    n_slot = 16 * quart_m
    units = wg.shape[1]
    gate = gate.reshape(16, 2, quart_m, units)[:, 0].reshape(n_slot, units)
    up = up.reshape(16, 2, quart_m, units)[:, 0].reshape(n_slot, units)
    back = back.reshape(16, 2, quart_m, units)[:, 1].reshape(n_slot, units)
    sig = jax.nn.sigmoid(gate)
    active = gate * sig
    hidden = (active * up).astype(BF16)
    gate_back = (back * up * sig * (1.0 + gate * (1.0 - sig))).astype(BF16)
    up_back = (back * active).astype(BF16)
    for cc in (other, c):
        for h in range(2):
            k0 = pl.multiple_of(cc * (2 * width) + h * width, 128)
            part_out = dot(hidden, wd[:, pl.ds(k0, width)])
            part_in = dot(gate_back, wgt[:, pl.ds(k0, width)]) + dot(up_back, wut[:, pl.ds(k0, width)])
            both = jnp.stack(
                [part_out.reshape(16, quart_m, width), part_in.reshape(16, quart_m, width)], axis=1
            ).reshape(16, half_m, width)
            obuf[cc, :, h * half_m:(h + 1) * half_m, :] = both.astype(BF16)
        if cc is other:
            for n, (lo_id, hi_id) in enumerate(((0, 6), (10, 16), (6, 10))):
                span = pl.ds(lo_id, hi_id - lo_id)
                sends.append(remote(obuf.at[other, span], pin.at[span], ps.at[n], pr.at[n], dev(y, x, z, other)))
                sends[-1].start()

    def pin_arrived(n):
        lo_id, hi_id = ((0, 6), (10, 16), (6, 10))[n]
        span = pl.ds(lo_id, hi_id - lo_id)
        remote(obuf.at[other, span], pin.at[span], ps.at[n], pr.at[n], dev(y, x, z, other)).wait_recv()

    def mine(i):
        return obuf[c, i].astype(F32) + pin[i].astype(F32)

    def out_left(i):
        return remote(cbuf.at[i], in_left.at[i], los.at[i], lor.at[i], dev(y, x, z_left, c))

    def out_right(i):
        return remote(cbuf.at[i], in_right.at[i - 6], ros.at[i - 6], ror.at[i - 6], dev(y, x, z_right, c))

    def out_final(i):
        dq = 1 if 2 <= i < 6 else 3 if 10 <= i < 14 else 2
        return remote(cbuf.at[i], fin.at[q], fs.at[i], fr.at[dq], dev(y, x, (4 * q + 10 + i) % NZ, c))

    pin_arrived(0)
    pin_arrived(1)
    for j in range(6):
        i = j

        @pl.when(r == 3)
        def _():
            cbuf[i] = mine(i).astype(BF16)
            out_left(i).start()

        @pl.when(r < 3)
        def _():
            out_left(i).wait_recv()
            cbuf[i] = (mine(i) + in_left[i].astype(F32)).astype(BF16)

            @pl.when(r > 0)
            def _():
                out_left(i).start()

            @pl.when(r == 0)
            def _():
                out_final(i).start()

        k = 15 - j

        @pl.when(r == 0)
        def _():
            cbuf[k] = mine(k).astype(BF16)
            out_right(k).start()

        @pl.when(r > 0)
        def _():
            out_right(k).wait_recv()
            cbuf[k] = (mine(k) + in_right[k - 6].astype(F32)).astype(BF16)

            @pl.when(r < 3)
            def _():
                out_right(k).start()

            @pl.when(r == 3)
            def _():
                out_final(k).start()

    pin_arrived(2)
    for n in range(4):
        i = 6 + n

        @pl.when(r == n)
        def _():
            total = mine(i)
            if n < 3:
                out_left(i).wait_recv()
                total = total + in_left[i].astype(F32)
            if n > 0:
                out_right(i).wait_recv()
                total = total + in_right[i - 6].astype(F32)
            fin[q] = total.astype(BF16)

        @pl.when(r > n)
        def _():
            @pl.when(r == 3)
            def _():
                cbuf[i] = mine(i).astype(BF16)

            @pl.when(r < 3)
            def _():
                out_left(i).wait_recv()
                cbuf[i] = (mine(i) + in_left[i].astype(F32)).astype(BF16)

            out_left(i).start()

        @pl.when(r < n)
        def _():
            @pl.when(r == 0)
            def _():
                cbuf[i] = mine(i).astype(BF16)

            @pl.when(r > 0)
            def _():
                out_right(i).wait_recv()
                cbuf[i] = (mine(i) + in_right[i - 6].astype(F32)).astype(BF16)

            out_right(i).start()

    for dq in range(1, 4):
        src = (q + dq) % 4
        remote(cbuf.at[0], fin.at[src], fs.at[0], fr.at[dq], dev(y, x, z_right, c)).wait_recv()

    rp[...] = dot(from_quad, fin[...].reshape(n_out, width)).astype(BF16).reshape(nx, 32, width)
    for d in range(1, nx):
        to = (x + d) % nx
        sends.append(remote(rp.at[to], ret.at[x], xbs.at[d], xbr.at[d], dev(y, to, z, c)))
        sends[-1].start()
    ret[x] = rp[x]
    for d in range(1, nx):
        src = (x + nx - d) % nx
        remote(rp.at[src], ret.at[src], xbs.at[d], xbr.at[d], dev(y, src, z, c)).wait_recv()

    returned = ret[...].reshape(n_out, width)
    ymsg[...] = dot(weight_matrix, returned).astype(BF16).reshape(ny, 16, width)
    for d in range(1, ny):
        to = (y + d) % ny
        sends.append(remote(ymsg.at[to], ybuf.at[y], ys.at[d], yr.at[d], dev(to, x, z, c)))
        sends[-1].start()
    ybuf[y] = ymsg[y]
    products = dot_nt(packed[...].reshape(n_out, width), returned)
    slot_score = jnp.sum(
        jnp.where((rm == cm + 2) & ((cm // 2) % 2 == 0), products, 0.0), axis=0, keepdims=True
    )
    token_score = jnp.where((select > 0.0) & ((lo // 2) % 2 == 0), slot_score, 0.0)
    lane = iota((n_in, 128), 1)
    scores = jnp.zeros((n_in, 128), F32)
    for k in range(top_k):
        of_pick = jnp.sum(jnp.where(known[:, k:k + 1] == target, token_score, 0.0), axis=1, keepdims=True)
        scores = jnp.where(lane == k, of_pick, scores)
    smsg[...] = scores.reshape(ny, 16, 128)[:, 0:8, :]
    for d in range(1, ny):
        to = (y + d) % ny
        for cc in range(2):
            sends.append(remote(
                smsg.at[to], sbuf.at[c, y], ss.at[2 * d + cc], sr.at[2 * d + c], dev(to, x, z, cc)
            ))
            sends[-1].start()
    sends.append(remote(smsg.at[y], sbuf.at[c, y], ss.at[0], sr.at[0], dev(y, x, z, other)))
    sends[-1].start()
    sbuf[c, y] = smsg[y]
    for d in range(1, ny):
        src = (y + ny - d) % ny
        remote(ymsg.at[src], ybuf.at[src], ys.at[d], yr.at[d], dev(src, x, z, c)).wait_recv()
    total = jnp.zeros((16, width), F32)
    for n in range(ny):
        total = total + ybuf[n].astype(F32)
    for h in range(2):
        mixed_ref[:, h * width:(h + 1) * width] = total[h * 8:h * 8 + 4].astype(BF16)
        grad_ref[:, h * width:(h + 1) * width] = total[h * 8 + 4:h * 8 + 8].astype(BF16)
    remote(smsg.at[y], sbuf.at[other, y], ss.at[0], sr.at[0], dev(y, x, z, other)).wait_recv()
    for d in range(1, ny):
        src = (y + ny - d) % ny
        for cc in range(2):
            remote(
                smsg.at[src], sbuf.at[cc, src], ss.at[2 * d + cc], sr.at[2 * d + cc], dev(src, x, z, cc)
            ).wait_recv()
    score = jnp.sum(sbuf[...].reshape(2 * ny, 8, 128), axis=0)[0:4]
    share = top_k // 2
    score_ref[...] = jnp.where(c == 0, score[:, 0:share], score[:, share:2 * share])

    for cp in sends:
        cp.wait_send()
    for i in range(16):
        to_core(i).wait_send()
        goes_right = r < 3 if i < 6 else (r < 3) & (r >= i - 6) if i < 10 else None
        goes_left = r > 0 if i >= 10 else (r > 0) & (r <= i - 6) if i >= 6 else None
        back_left = r > 0 if i < 6 else r > i - 6 if i < 10 else None
        back_right = r < 3 if i >= 10 else r < i - 6 if i >= 6 else None
        for cond, cp in ((goes_right, to_right), (goes_left, to_left), (back_left, out_left), (back_right, out_right)):
            if cond is not None:
                @pl.when(cond)
                def _():
                    cp(i).wait_send()
        if i < 6 or i >= 10:
            @pl.when(r == (0 if i < 6 else 3))
            def _():
                out_final(i).wait_send()


def body(tokens, cotangent, group_ids, expert_ids, gate_weights, w_gate, w_up, w_down):
    ny = lax.axis_size("group")
    nx = lax.axis_size("expert") // NZ
    depth = tokens.shape[1]
    units = w_gate.shape[2]
    width = depth // 4
    rows_m = 8 * nx
    dma = pltpu.SemaphoreType.DMA
    vmem = pl.BlockSpec(memory_space=pltpu.VMEM)
    hbm = pl.BlockSpec(memory_space=pl.ANY)

    def buf(*shape):
        return pltpu.VMEM(shape, BF16)

    scratch = [
        buf(depth, units), buf(depth, units), buf(units, depth),
        buf(depth, units), buf(units, depth), buf(units, depth),
        pltpu.VMEM((16, width), F32), buf(ny, 16, width), pltpu.VMEM((ny, 8, 128), F32),
        buf(nx, 32, width), buf(nx, 32, width), buf(4, rows_m, width),
        buf(2, 16, rows_m, width), buf(2, 16, rows_m, width), buf(16, rows_m, width), buf(16, rows_m, width),
        buf(10, rows_m, width), buf(10, rows_m, width),
        buf(4, rows_m, width), buf(nx, 32, width), buf(nx, 32, width),
        buf(ny, 16, width), buf(ny, 16, width),
        pltpu.VMEM((ny, 8, 128), F32), pltpu.VMEM((2, ny, 8, 128), F32),
        dma((3,)), dma((ny,)), dma((ny,)), dma((ny,)), dma((ny,)),
        dma((nx,)), dma((nx,)), dma((3,)), dma((16,)), dma((16,)), dma((16,)), dma((16,)), dma((16,)),
        dma((3,)), dma((3,)),
        dma((10,)), dma((10,)), dma((10,)), dma((10,)), dma((16,)), dma((4,)),
        dma((nx,)), dma((nx,)), dma((ny,)), dma((ny,)), dma((2 * ny,)), dma((2 * ny,)),
    ]
    return pl.pallas_call(
        functools.partial(kernel, ny, nx, 4 * nx),
        out_shape=(
            jax.ShapeDtypeStruct((tokens.shape[0], depth // 2), BF16),
            jax.ShapeDtypeStruct((tokens.shape[0], depth // 2), BF16),
            jax.ShapeDtypeStruct((tokens.shape[0], expert_ids.shape[1] // 2), F32),
        ),
        in_specs=[vmem] * 5 + [hbm] * 3,
        out_specs=(vmem, vmem, vmem),
        scratch_shapes=scratch,
        compiler_params=pltpu.CompilerParams(
            collective_id=0, has_side_effects=True, vmem_limit_bytes=40 * 1024 * 1024
        ),
    )(tokens, cotangent, group_ids, expert_ids, gate_weights, w_gate, w_up, w_down)


def solution(mesh):
    rows = P(("group", "expert"), None)
    return jax.shard_map(
        body,
        mesh=mesh,
        in_specs=(
            rows, rows, rows, rows, rows,
            P(("group", "expert"), None, "ffn"),
            P(("group", "expert"), None, "ffn"),
            P(("group", "expert"), "ffn", None),
        ),
        out_specs=(
            P(("group", "expert"), "ffn"),
            P(("group", "expert"), "ffn"),
            P(("group", "expert"), "ffn"),
        ),
        check_vma=False,
    )
```

time: 352 us -> 316 us (0.90); the launches traced: 350 us -> 309 us
  Pallas kernels: 0 us -> 300 us
  waiting for transfers between devices: 211 us -> 0 us
  starting transfers between devices: 77.3 us -> 0 us
  blocking collectives: 24.7 us -> 0 us
  local copies, waits for them, and re-layouts: 21.4 us -> 8.84 us
  other arithmetic: 8.84 us -> 0 us
  matrix products: 5.77 us -> 0 us
    pallas_call x0 -> x1, Pallas kernels: none -> 300 us  [body(): pl.pallas_call(functools.partial(kernel, ny, nx, 4 * nx), out_shape=(jax....]
    all_to_all x10 -> x0, waiting for transfers between devices: 211 us -> none  [the longest x1 41.2 us: body(): lax.all_to_all(outgoing_rows, 'expert', split_axis=0, concat_axis=0, tile...]
    all_to_all x10 -> x0, starting transfers between devices: 77.3 us -> none  [the longest x1 20.4 us: body(): lax.all_to_all(outgoing_rows, 'expert', split_axis=0, concat_axis=0, tile...]
    all_to_all x1 -> x0, blocking collectives: 24.7 us -> none  [body(): lax.all_to_all(inner_score, 'expert', split_axis=0, concat_axis=0, tiled=...]
    convert_element_type x11 -> x0, local copies, waits for them, and re-layouts: 11.8 us -> none  [the longest x1 3.21 us: body(): jnp.einsum('gixc,xscfh->gfih', weighted, back_out, preferred_element_type...]
    unnamed x16 -> x19, local copies, waits for them, and re-layouts: 2.81 us -> 8.84 us
    dot_general x12 -> x0, matrix products: 5.77 us -> none  [the longest x1 1.65 us: body(): jnp.einsum('slcd,ldh->slch', rows_in, w_gate, preferred_element_type=jnp....]
    reduce_sum x7 -> x0, other arithmetic: 3.79 us -> none  [the longest x1 1.12 us: body(): jnp.einsum('gixc,xscfh->gfih', weighted, back_out, preferred_element_type...]
  transfers between devices with their start and end apart: 10 -> 0, of which waited for: 10 -> 0; matrix products, arithmetic and copies ran while one was open for 7% -> 0% of each run, Pallas kernels for 0% -> 0%
where the time goes in v1:
time: 316 us; the launch traced here: 309 us
  Pallas kernels  300 us (95%)
  local copies, waits for them, and re-layouts  8.84 us (3%)
    pallas_call x1, Pallas kernels, body(): pl.pallas_call(functools.partial(kernel, ny, nx, 4 * nx), out_shape=(jax....  300 us
    unnamed x19, local copies, waits for them, and re-layouts  8.84 us

profile of v1, /device:TPU:1, one launch (start us, length us, event | category | flops | bytes accessed | tf_op | source)
XLA Modules:
  0.0 309.2 jit_solution(4394170102061903082)
XLA Ops:
  0.6 0.0 copy-start
  0.6 1.2 copy-done
  1.8 0.0 copy-start.1
  1.8 1.2 copy-done.1
  3.0 0.0 copy-start.2
  3.0 1.2 copy-done.2
  4.2 0.0 copy-start.3
  4.2 0.7 copy-done.3
  4.9 0.0 copy-start.4
  4.9 0.7 copy-done.4
  5.7 0.0 copy-start.5
  5.7 0.7 copy-done.5
  6.4 0.0 copy-start.6
  6.4 0.7 copy-done.6
  7.0 0.0 copy-start.7
  7.0 0.7 copy-done.7
  7.7 299.7 %shard_map.103 = (bf16[4,1792]{1,0:T(4,128)(2,1)S(1)}, bf16[4,1792]{1,0:T(4,128)(2,1)S(1)}, f32[4,4]{1,0:T(4,128)S(1)}) custom-call(bf16[4,3584]{1,0:T(4,128)(2,1)S(1)} %copy-done.3, bf16[4,3584]{1,0:T(4,128)(2,1)S(1)} %copy-done.4, s32[4,4]{1,0:T(4,128)S(1)} %copy-done.5, s32[4,8]{1,0:T(4,128)S(1)} %copy-done.6, bf16[4,8]{1,0:T(4,128)(2,1)S(1)} %copy-done.7, ...), custom_call_target="tpu_custom_call" | custom-call | tf_op jit(solution)/shard_map/pallas_call | solution.py:501
  307.5 0.6 copy.14
  308.1 0.6 copy.15
  308.7 0.6 copy.16
Async XLA Ops:
  0.6 1.2 copy-start
  1.8 1.2 copy-start.1
  3.0 1.2 copy-start.2
  4.2 0.7 copy-start.3
  4.9 0.7 copy-start.4
  5.7 0.7 copy-start.5
  6.4 0.7 copy-start.6
  7.0 0.7 copy-start.7

commit v2 on v1

v2 whole, which is shorter than its diff:
```python
import functools

import jax
import jax.numpy as jnp
from jax import lax
from jax.experimental import pallas as pl
from jax.experimental.pallas import tpu as pltpu
from jax.sharding import PartitionSpec as P

NZ = 16
RELAY_HOP = 7
RELAY_GAP = 5
COLLECT_HOP = 4
COLLECT_GAP = 5
FINISH_HOP = 4
MESH = pl.DeviceIdType.MESH
F32 = jnp.float32
BF16 = jnp.bfloat16


def iota(shape, dim):
    return lax.broadcasted_iota(jnp.int32, shape, dim)


def dot(a, b):
    return jnp.dot(a, b, preferred_element_type=F32)


def dot_nt(a, b):
    return lax.dot_general(a, b, (((1,), (1,)), ((), ())), preferred_element_type=F32)


def kernel(
    ny, nx, per_group,
    tok_hbm, cot_hbm, gid_hbm, eid_hbm, gw_hbm, wg_hbm, wu_hbm, wd_hbm,
    mixed_hbm, grad_hbm, score_hbm,
    tok_ref, cot_ref, gid_ref, eid_ref, gw_ref, mixed_ref, grad_ref, score_ref,
    wg, wu, wd, wdt, wgt, wut,
    msg32, gbuf, ibuf, packed, xbuf, mbuf, zbuf, obuf, pin, cbuf, in_left, in_right,
    fin, rp, ret, ymsg, ybuf, smsg, sbuf, half_score, whole_score,
    asem, osem, wsem, gs, gr, isem, ir, xs, xr, zds, zr, zfr, zfl, cs, cr, ps, pr,
    los, lor, ros, ror, fs, fr, xbs, xbr, ys, yr, ss, sr, hs, hr,
):
    y = lax.axis_index("group")
    e = lax.axis_index("expert")
    c = lax.axis_index("ffn")
    x = e // NZ
    z = e % NZ
    q = z // 4
    r = z % 4
    other = 1 - c
    width = msg32.shape[1]
    top_k = eid_ref.shape[1]
    rows_m = mbuf.shape[1]
    half_m = rows_m // 2
    quart_m = rows_m // 4
    n_in = ny * 16
    n_out = nx * 32
    first = (width // 128 + 1) // 2 * 128
    chunks = (pl.ds(0, first), pl.ds(first, width - first))
    both_chunks = range(2)

    def dev(yy, xx, zz, cc):
        return (yy, xx * NZ + zz, cc)

    def remote(src, dst, send, recv, where):
        return pltpu.make_async_remote_copy(
            src_ref=src, dst_ref=dst, send_sem=send, recv_sem=recv,
            device_id=where, device_id_type=MESH,
        )

    inputs = [
        pltpu.make_async_copy(src, dst, asem.at[k])
        for k, (src, dst) in enumerate((
            (tok_hbm, tok_ref), (cot_hbm, cot_ref), (gid_hbm, gid_ref), (eid_hbm, eid_ref), (gw_hbm, gw_ref),
        ))
    ]
    for cp in inputs:
        cp.start()

    weight_copies = [
        pltpu.make_async_copy(wg_hbm.at[0], wg, wsem.at[0]),
        pltpu.make_async_copy(wu_hbm.at[0], wu, wsem.at[1]),
        pltpu.make_async_copy(wd_hbm.at[0], wd, wsem.at[2]),
    ]
    for cp in weight_copies:
        cp.start()

    barrier = pltpu.get_barrier_semaphore()
    q1 = (q + 1) % 4
    q2 = (q + 2) % 4
    q3 = (q + 3) % 4
    end2 = jnp.where(r >= 2, 0, 3)
    z_right = (z + 1) % NZ
    z_left = (z + NZ - 1) % NZ

    def greet(where):
        pl.semaphore_signal(barrier, inc=1, device_id=where, device_id_type=MESH)

    greet(dev(y, x, z, other))
    for d in range(1, ny):
        greet(dev((y + d) % ny, x, z, c))
    for d in range(1, nx):
        greet(dev(y, (x + d) % nx, z, c))

    def greet_z(d):
        greet(dev(y, x, (z + NZ + d) % NZ, c))

    @pl.when(r == 0)
    def _():
        for d in (1, 4, -1, -2, -3, -4, -5, -6):
            greet_z(d)

    @pl.when(r == 3)
    def _():
        for d in (-1, -4, 1, 2, 3, 4, 5, 6):
            greet_z(d)

    @pl.when((r == 1) | (r == 2))
    def _():
        greet_z(1)
        greet_z(-1)
        greet(dev(y, x, 4 * q1, c))
        greet(dev(y, x, 4 * q2 + end2, c))
        greet(dev(y, x, 4 * q3 + 3, c))

    for cp in inputs:
        cp.wait()

    for h in range(2):
        for a, ref in enumerate((tok_ref, cot_ref)):
            start = pl.multiple_of(c * (2 * width) + h * width, 128)
            msg32[h * 8 + a * 4:h * 8 + a * 4 + 4, :] = ref[:, pl.ds(start, width)].astype(F32)
    gbuf[y] = msg32[...].astype(BF16)
    lane4 = iota((4, 128), 1)
    gid = gid_ref[...].astype(F32)
    eid = eid_ref[...].astype(F32)
    gw = gw_ref[...].astype(F32)
    info = jnp.zeros((4, 128), F32)
    for k in range(top_k):
        ident = gid[:, k // 2:k // 2 + 1] * float(per_group) + eid[:, k:k + 1]
        info = jnp.where(lane4 == k, ident, info)
        info = jnp.where(lane4 == top_k + k, gw[:, k:k + 1], info)
    ibuf[y] = jnp.full((8, 128), -1.0, F32)
    ibuf[y, 0:4, :] = info

    pl.semaphore_wait(barrier, ny + nx - 1 + jnp.where((r == 0) | (r == 3), 8, 5))

    def gather_info(d, to, src):
        return remote(ibuf.at[src], ibuf.at[src], isem.at[d], ir.at[d], dev(to, x, z, c))

    def gather_rows(d, n, to, src):
        part = gbuf.at[src, :, chunks[n]]
        return remote(part, part, gs.at[n, d], gr.at[n, d], dev(to, x, z, c))

    sends = []

    def send(cp):
        cp.start()
        sends.append(cp)

    for d in range(1, ny):
        send(gather_info(d, (y + d) % ny, y))
    for n in both_chunks:
        for d in range(1, ny):
            send(gather_rows(d, n, (y + d) % ny, y))

    for cp in weight_copies:
        cp.wait()

    def turn(i, carry):
        at = pl.ds(pl.multiple_of(i * 128, 128), 128)
        wgt[:, at] = wg[at, :].T
        wut[:, at] = wu[at, :].T
        wdt[at, :] = wd[:, at].T
        return carry

    lax.fori_loop(0, wg.shape[0] // 128, turn, 0)

    for d in range(1, ny):
        src = (y + ny - d) % ny
        gather_info(d, src, src).wait_recv()

    n_tok = ny * 8
    known = ibuf[...].reshape(n_tok, 128)
    lo = iota((n_tok, n_out), 1)
    target = (y * per_group + (lo // 32) * 4 + (lo // 4) % 4).astype(F32)
    picked = jnp.zeros((n_tok, n_out), F32)
    weight = jnp.zeros((n_tok, n_out), F32)
    for k in range(top_k):
        hit = known[:, k:k + 1] == target
        picked = jnp.where(hit, 1.0, picked)
        weight = jnp.where(hit, known[:, top_k + k:top_k + k + 1], weight)
    earlier = (iota((n_tok, n_tok), 1) < iota((n_tok, n_tok), 0)).astype(F32).astype(BF16)
    before = dot(earlier, picked.astype(BF16))
    select = jnp.where((before == (lo % 2).astype(F32)) & (picked > 0.0), 1.0, 0.0)
    row_e = iota((n_in, n_tok), 0)
    col_e = iota((n_in, n_tok), 1)
    expand = ((row_e // 16 == col_e // 8) & (row_e % 4 == col_e % 8)).astype(F32).astype(BF16)
    ri = iota((n_in, n_out), 0)
    li = iota((n_in, n_out), 1)
    same = ((ri // 4) % 2 == (li // 2) % 2) & ((ri // 8) % 2 == (li // 16) % 2)
    pick_matrix = jnp.where(same, dot(expand, select.astype(BF16)), 0.0).T.astype(BF16)
    weight_matrix = jnp.where(same, dot(expand, (select * weight).astype(BF16)), 0.0).astype(BF16)

    rm = iota((n_out, n_out), 0)
    cm = iota((n_out, n_out), 1)

    def x_row(m):
        return ((m // 2) % nx) * 32 + ((m // half_m) % 2) * 16 + (m // rows_m) * 4 + ((m // quart_m) % 2) * 2 + m % 2

    to_quad = (cm == x_row(rm)).astype(F32).astype(BF16)
    from_quad = (rm == x_row(cm)).astype(F32).astype(BF16)

    def x_out(d, n, to, src):
        return remote(
            packed.at[to, :, chunks[n]], xbuf.at[src, :, chunks[n]], xs.at[n, d], xr.at[n, d], dev(y, to, z, c)
        )

    for n in both_chunks:
        for d in range(1, ny):
            src = (y + ny - d) % ny
            gather_rows(d, n, src, src).wait_recv()
        rows = gbuf[:, :, chunks[n]].reshape(n_in, chunks[n].size)
        packed[:, :, chunks[n]] = dot(pick_matrix, rows).astype(BF16).reshape(nx, 32, chunks[n].size)
        for d in range(1, nx):
            send(x_out(d, n, (x + d) % nx, x))
        xbuf[x, :, chunks[n]] = packed[x, :, chunks[n]]

    own = 6 + r
    id2 = (r + 14) % 16

    def along(i, n, sem, to):
        part = zbuf.at[c, i, :, chunks[n]]
        return remote(part, part, sem.at[n, i], zr.at[n, i], dev(y, x, to, c))

    def to_right(i, n):
        return along(i, n, zfr, z_right)

    def to_left(i, n):
        return along(i, n, zfl, z_left)

    def across(i, n, half):
        part = zbuf.at[half, i, :, chunks[n]]
        return remote(part, part, cs.at[n, i], cr.at[n, i], dev(y, x, z, other))

    def enter(n, k, quad, slot, where):
        return remote(
            mbuf.at[quad, :, chunks[n]], zbuf.at[c, slot, :, chunks[n]], zds.at[n, k], zr.at[n, slot],
            dev(y, x, where, c),
        )

    for n in both_chunks:
        for d in range(1, nx):
            src = (x + nx - d) % nx
            x_out(d, n, src, src).wait_recv()
        rows = xbuf[:, :, chunks[n]].reshape(n_out, chunks[n].size)
        mbuf[:, :, chunks[n]] = dot(to_quad, rows).astype(BF16).reshape(4, rows_m, chunks[n].size)
        zbuf[c, own, :, chunks[n]] = mbuf[q, :, chunks[n]]

        @pl.when(r < 3)
        def _():
            to_right(own, n).start()

        @pl.when(r > 0)
        def _():
            to_left(own, n).start()

        send(enter(n, 1, q1, r + 2, 4 * q1))
        send(enter(n, 2, q3, r + 10, 4 * q3 + 3))
        send(enter(n, 0, q2, id2, 4 * q2 + end2))
        across(own, n, c).start()

    def relay(t, carry):
        for n in both_chunks:
            u = t - n * RELAY_GAP
            for rank, step, ends, onward in ((r, -1, r < 3, to_right), (3 - r, 1, r > 0, to_left)):
                near = (u >= 1) & (u <= RELAY_HOP * rank) & (u % RELAY_HOP == 0)
                late = u - RELAY_HOP * (rank + 1)
                far = (late >= 0) & (late < 6)
                i = own + step * jnp.where(near, u // RELAY_HOP, rank + 1 + late)

                @pl.when(near | far)
                def _():
                    onward(i, n).wait_recv()

                    @pl.when(ends)
                    def _():
                        onward(i, n).start()

                    across(i, n, c).start()

        return carry

    lax.fori_loop(1, RELAY_GAP + 4 * RELAY_HOP + 6, relay, 0)

    def other_half(i, carry):
        for n in both_chunks:
            across(i, n, other).wait_recv()
        return carry

    lax.fori_loop(0, 16, other_half, 0)

    gate = up = back = None
    for cc in range(2):
        for h in range(2):
            rows = zbuf[cc, :, h * half_m:(h + 1) * half_m, :].reshape(16 * half_m, width)
            k0 = (2 * cc + h) * width
            parts = [dot(rows, w[k0:k0 + width, :]) for w in (wg, wu, wdt)]
            if gate is None:
                gate, up, back = parts
            else:
                gate, up, back = gate + parts[0], up + parts[1], back + parts[2]
    n_slot = 16 * quart_m
    units = wg.shape[1]
    gate = gate.reshape(16, 2, quart_m, units)[:, 0].reshape(n_slot, units)
    up = up.reshape(16, 2, quart_m, units)[:, 0].reshape(n_slot, units)
    back = back.reshape(16, 2, quart_m, units)[:, 1].reshape(n_slot, units)
    sig = jax.nn.sigmoid(gate)
    active = gate * sig
    hidden = (active * up).astype(BF16)
    gate_back = (back * up * sig * (1.0 + gate * (1.0 - sig))).astype(BF16)
    up_back = (back * active).astype(BF16)

    def partner_sum(n):
        return remote(
            obuf.at[other, :, :, chunks[n]], pin.at[:, :, chunks[n]], ps.at[n], pr.at[n], dev(y, x, z, other)
        )

    for n in both_chunks:
        size = chunks[n].size
        for half in (other, c):
            for h in range(2):
                at = pl.ds(pl.multiple_of(half * (2 * width) + h * width + chunks[n].start, 128), size)
                part_out = dot(hidden, wd[:, at])
                part_in = dot(gate_back, wgt[:, at]) + dot(up_back, wut[:, at])
                both = jnp.stack(
                    [part_out.reshape(16, quart_m, size), part_in.reshape(16, quart_m, size)], axis=1
                ).reshape(16, half_m, size)
                obuf[half, :, h * half_m:(h + 1) * half_m, chunks[n]] = both.astype(BF16)
            if half is other:
                send(partner_sum(n))

    def mine(i, n):
        return obuf[c, i, :, chunks[n]].astype(F32) + pin[i, :, chunks[n]].astype(F32)

    def out_left(i, n):
        return remote(
            cbuf.at[i, :, chunks[n]], in_left.at[i, :, chunks[n]], los.at[n, i], lor.at[n, i], dev(y, x, z_left, c)
        )

    def out_right(i, n):
        return remote(
            cbuf.at[i, :, chunks[n]], in_right.at[i - 6, :, chunks[n]], ros.at[n, i - 6], ror.at[n, i - 6],
            dev(y, x, z_right, c),
        )

    def out_final(i, n, dq):
        return remote(
            cbuf.at[i, :, chunks[n]], fin.at[q, :, chunks[n]], fs.at[n, i], fr.at[n, dq],
            dev(y, x, (4 * q + 10 + i) % NZ, c),
        )

    def collect(t, carry):
        for n in both_chunks:
            u = t - n * COLLECT_GAP
            for rank, step, outward, landed in ((3 - r, 1, out_left, in_left), (r, -1, out_right, in_right)):
                k = u - COLLECT_HOP * rank
                i = k if step == 1 else 15 - k
                slot = i if step == 1 else i - 6

                @pl.when((k >= 0) & (k < 9 - rank))
                def _():
                    @pl.when(rank == 0)
                    def _():
                        cbuf[i, :, chunks[n]] = mine(i, n).astype(BF16)

                    @pl.when(rank > 0)
                    def _():
                        outward(i, n).wait_recv()
                        cbuf[i, :, chunks[n]] = (mine(i, n) + landed[slot, :, chunks[n]].astype(F32)).astype(BF16)

                    @pl.when(rank < 3)
                    def _():
                        outward(i, n).start()

                    @pl.when(rank == 3)
                    def _():
                        out_final(i, n, jnp.where(k < 2, 2, 2 - step)).start()

        return carry

    def finish_own(n):
        @pl.when(r == 0)
        def _():
            out_left(own, n).wait_recv()
            fin[q, :, chunks[n]] = (mine(own, n) + in_left[own, :, chunks[n]].astype(F32)).astype(BF16)

        @pl.when(r == 3)
        def _():
            out_right(own, n).wait_recv()
            fin[q, :, chunks[n]] = (mine(own, n) + in_right[r, :, chunks[n]].astype(F32)).astype(BF16)

        @pl.when((r > 0) & (r < 3))
        def _():
            out_left(own, n).wait_recv()
            out_right(own, n).wait_recv()
            fin[q, :, chunks[n]] = (
                mine(own, n) + in_left[own, :, chunks[n]].astype(F32) + in_right[r, :, chunks[n]].astype(F32)
            ).astype(BF16)

    def x_back(d, n, to, src):
        return remote(
            rp.at[to, :, chunks[n]], ret.at[src, :, chunks[n]], xbs.at[n, d], xbr.at[n, d], dev(y, to, z, c)
        )

    def finish_z(n):
        finish_own(n)
        for dq in range(1, 4):
            part = fin.at[(q + dq) % 4, :, chunks[n]]
            remote(part, part, fs.at[n, 0], fr.at[n, dq], dev(y, x, z_right, c)).wait_recv()
        rows = fin[:, :, chunks[n]].reshape(n_out, chunks[n].size)
        rp[:, :, chunks[n]] = dot(from_quad, rows).astype(BF16).reshape(nx, 32, chunks[n].size)
        for d in range(1, nx):
            send(x_back(d, n, (x + d) % nx, x))
        ret[x, :, chunks[n]] = rp[x, :, chunks[n]]

    def y_back(d, n, to, src):
        return remote(
            ymsg.at[to, :, chunks[n]], ybuf.at[src, :, chunks[n]], ys.at[n, d], yr.at[n, d], dev(to, x, z, c)
        )

    def finish_x(n):
        for d in range(1, nx):
            src = (x + nx - d) % nx
            x_back(d, n, src, src).wait_recv()
        rows = ret[:, :, chunks[n]].reshape(n_out, chunks[n].size)
        ymsg[:, :, chunks[n]] = dot(weight_matrix, rows).astype(BF16).reshape(ny, 16, chunks[n].size)
        for d in range(1, ny):
            send(y_back(d, n, (y + d) % ny, y))
        ybuf[y, :, chunks[n]] = ymsg[y, :, chunks[n]]
        return dot_nt(packed[:, :, chunks[n]].reshape(n_out, chunks[n].size), rows)

    partner_sum(0).wait_recv()
    partner_sum(1).wait_recv()
    first_done = 9 + 3 * COLLECT_HOP + FINISH_HOP
    last = COLLECT_GAP + 9 + 3 * COLLECT_HOP
    lax.fori_loop(0, first_done, collect, 0)
    finish_z(0)
    lax.fori_loop(first_done, first_done + FINISH_HOP, collect, 0)
    products = finish_x(0)
    if last > first_done + FINISH_HOP:
        lax.fori_loop(first_done + FINISH_HOP, last, collect, 0)
    finish_z(1)
    products = products + finish_x(1)

    slot_score = jnp.sum(
        jnp.where((rm == cm + 2) & ((cm // 2) % 2 == 0), products, 0.0), axis=0, keepdims=True
    )
    token_score = jnp.where((select > 0.0) & ((lo // 2) % 2 == 0), slot_score, 0.0)
    lane = iota((n_tok, 128), 1)
    scores = jnp.zeros((n_tok, 128), F32)
    for k in range(top_k):
        of_pick = jnp.sum(jnp.where(known[:, k:k + 1] == target, token_score, 0.0), axis=1, keepdims=True)
        scores = jnp.where(lane == k, of_pick, scores)
    smsg[...] = scores.reshape(ny, 8, 128)

    def score_back(d, to, src):
        return remote(smsg.at[to], sbuf.at[src], ss.at[d], sr.at[d], dev(to, x, z, c))

    for d in range(1, ny):
        send(score_back(d, (y + d) % ny, y))
    sbuf[y] = smsg[y]
    for d in range(1, ny):
        src = (y + ny - d) % ny
        score_back(d, src, src).wait_recv()
    half_score[...] = jnp.sum(sbuf[...], axis=0)
    to_partner = remote(half_score, whole_score, hs.at[0], hr.at[0], dev(y, x, z, other))
    send(to_partner)
    for n in both_chunks:
        for d in range(1, ny):
            src = (y + ny - d) % ny
            y_back(d, n, src, src).wait_recv()
    total = jnp.zeros((16, width), F32)
    for n in range(ny):
        total = total + ybuf[n].astype(F32)
    for h in range(2):
        mixed_ref[:, h * width:(h + 1) * width] = total[h * 8:h * 8 + 4].astype(BF16)
        grad_ref[:, h * width:(h + 1) * width] = total[h * 8 + 4:h * 8 + 8].astype(BF16)
    to_partner.wait_recv()
    score = (half_score[...] + whole_score[...])[0:4]
    outputs = [
        pltpu.make_async_copy(src, dst, osem.at[k])
        for k, (src, dst) in enumerate(((mixed_ref, mixed_hbm), (grad_ref, grad_hbm), (score_ref, score_hbm)))
    ]
    outputs[0].start()
    outputs[1].start()
    share = top_k // 2
    score_ref[...] = jnp.where(c == 0, score[:, 0:share], score[:, share:2 * share])
    outputs[2].start()

    for cp in sends:
        cp.wait_send()

    def sent(i, carry):
        near_right = (i >= 6) & (r >= i - 6) | (i < 6)
        near_left = (i < 10) & (r <= i - 6) | (i >= 10)
        for n in both_chunks:
            across(i, n, c).wait_send()

            @pl.when((r < 3) & near_right)
            def _():
                to_right(i, n).wait_send()

            @pl.when((r > 0) & near_left)
            def _():
                to_left(i, n).wait_send()

            @pl.when((r > 0) & (i < 6) | (i >= 6) & (r > i - 6))
            def _():
                out_left(i, n).wait_send()

            @pl.when((r < 3) & (i >= 10) | (i < 10) & (r < i - 6))
            def _():
                out_right(i, n).wait_send()

            @pl.when((r == 0) & (i < 6) | (r == 3) & (i >= 10))
            def _():
                out_final(i, n, 1).wait_send()

        return carry

    lax.fori_loop(0, 16, sent, 0)
    for cp in outputs:
        cp.wait()


def body(tokens, cotangent, group_ids, expert_ids, gate_weights, w_gate, w_up, w_down):
    ny = lax.axis_size("group")
    nx = lax.axis_size("expert") // NZ
    depth = tokens.shape[1]
    units = w_gate.shape[2]
    width = depth // 4
    rows_m = 8 * nx
    dma = pltpu.SemaphoreType.DMA
    hbm = pl.BlockSpec(memory_space=pl.ANY)

    def buf(*shape):
        return pltpu.VMEM(shape, BF16)

    n_tok, n_pick = expert_ids.shape
    small = [
        pltpu.VMEM(tokens.shape, BF16), pltpu.VMEM(cotangent.shape, BF16),
        pltpu.VMEM(group_ids.shape, jnp.int32), pltpu.VMEM(expert_ids.shape, jnp.int32),
        pltpu.VMEM(gate_weights.shape, BF16),
        pltpu.VMEM((n_tok, depth // 2), BF16), pltpu.VMEM((n_tok, depth // 2), BF16),
        pltpu.VMEM((n_tok, n_pick // 2), F32),
    ]
    scratch = small + [
        buf(depth, units), buf(depth, units), buf(units, depth),
        buf(depth, units), buf(units, depth), buf(units, depth),
        pltpu.VMEM((16, width), F32), buf(ny, 16, width), pltpu.VMEM((ny, 8, 128), F32),
        buf(nx, 32, width), buf(nx, 32, width), buf(4, rows_m, width),
        buf(2, 16, rows_m, width), buf(2, 16, rows_m, width), buf(16, rows_m, width), buf(16, rows_m, width),
        buf(10, rows_m, width), buf(10, rows_m, width),
        buf(4, rows_m, width), buf(nx, 32, width), buf(nx, 32, width),
        buf(ny, 16, width), buf(ny, 16, width),
        pltpu.VMEM((ny, 8, 128), F32), pltpu.VMEM((ny, 8, 128), F32),
        pltpu.VMEM((8, 128), F32), pltpu.VMEM((8, 128), F32),
        dma((5,)), dma((3,)), dma((3,)), dma((2, ny)), dma((2, ny)), dma((ny,)), dma((ny,)),
        dma((2, nx)), dma((2, nx)), dma((2, 3)), dma((2, 16)), dma((2, 16)), dma((2, 16)), dma((2, 16)), dma((2, 16)),
        dma((2,)), dma((2,)),
        dma((2, 10)), dma((2, 10)), dma((2, 10)), dma((2, 10)), dma((2, 16)), dma((2, 4)),
        dma((2, nx)), dma((2, nx)), dma((2, ny)), dma((2, ny)), dma((ny,)), dma((ny,)), dma((1,)), dma((1,)),
    ]
    return pl.pallas_call(
        functools.partial(kernel, ny, nx, 4 * nx),
        out_shape=(
            jax.ShapeDtypeStruct((tokens.shape[0], depth // 2), BF16),
            jax.ShapeDtypeStruct((tokens.shape[0], depth // 2), BF16),
            jax.ShapeDtypeStruct((tokens.shape[0], expert_ids.shape[1] // 2), F32),
        ),
        in_specs=[hbm] * 8,
        out_specs=(hbm, hbm, hbm),
        scratch_shapes=scratch,
        compiler_params=pltpu.CompilerParams(
            collective_id=0, has_side_effects=True, vmem_limit_bytes=60 * 1024 * 1024
        ),
    )(tokens, cotangent, group_ids, expert_ids, gate_weights, w_gate, w_up, w_down)


def solution(mesh):
    rows = P(("group", "expert"), None)
    return jax.shard_map(
        body,
        mesh=mesh,
        in_specs=(
            rows, rows, rows, rows, rows,
            P(("group", "expert"), None, "ffn"),
            P(("group", "expert"), None, "ffn"),
            P(("group", "expert"), "ffn", None),
        ),
        out_specs=(
            P(("group", "expert"), "ffn"),
            P(("group", "expert"), "ffn"),
            P(("group", "expert"), "ffn"),
        ),
        check_vma=False,
    )
```

time: 316 us -> 107 us (0.34); the launches traced: 309 us -> 107 us
  Pallas kernels: 300 us -> 103 us
  local copies, waits for them, and re-layouts: 8.84 us -> 2.57 us
    pallas_call x1, Pallas kernels: 300 us -> 103 us  [body(): pl.pallas_call(functools.partial(kernel, ny, nx, 4 * nx), out_shape=(jax....]
    unnamed x19 -> x7, local copies, waits for them, and re-layouts: 8.84 us -> 2.57 us
where the time goes in v2:
time: 107 us
  Pallas kernels  103 us (96%)
  local copies, waits for them, and re-layouts  2.57 us (2%)
    pallas_call x1, Pallas kernels, body(): pl.pallas_call(functools.partial(kernel, ny, nx, 4 * nx), out_shape=(jax....  103 us
    unnamed x7, local copies, waits for them, and re-layouts  2.57 us

profile of v2, /device:TPU:1, one launch (start us, length us, event | category | flops | bytes accessed | tf_op | source)
XLA Modules:
  0.0 106.5 jit_solution(5278315618882152902)
XLA Ops:
  0.6 103.3 %shard_map.103 = (bf16[4,1792]{1,0:T(4,128)(2,1)}, bf16[4,1792]{1,0:T(4,128)(2,1)}, f32[4,4]{1,0:T(4,128)}) custom-call(bf16[4,3584]{1,0:T(4,128)(2,1)} %tok_hbm.1, bf16[4,3584]{1,0:T(4,128)(2,1)} %cot_hbm.1, s32[4,4]{1,0:T(4,128)} %gid_hbm.1, s32[4,8]{1,0:T(4,128)} %eid_hbm.1, bf16[4,8]{1,0:T(4,128)(2,1)} %gw_hbm.1, bf16[1,3584,128]{2,1,0:T(8,128)(2,1)} %wg_hbm.1, ...), custom_call_target="tpu_custom_call" | custom-call | tf_op jit(solution)/shard_map/pallas_call | solution.py:576
  103.9 0.0 copy-start
  103.9 1.3 %copy.14 = bf16[4,1792]{1,0:T(4,128)(2,1)} copy(bf16[4,1792]{1,0:T(4,128)(2,1)} %get-tuple-element.6) | data formatting | bytes 28672
  105.3 0.0 copy-done
  105.3 0.0 copy-start.1
  105.3 0.6 copy.15
  105.9 0.1 copy-done.1
  105.9 0.6 copy.16
Async XLA Ops:
  103.9 1.3 %copy-start = (bf16[4,1792]{1,0:T(4,128)(2,1)S(1)}, bf16[4,1792]{1,0:T(4,128)(2,1)}, u32[]{:S(2)}) copy-start(bf16[4,1792]{1,0:T(4,128)(2,1)} %get-tuple-element.7) | copy-start | bytes 43012
  105.3 0.7 copy-start.1

commit v3 on v2

--- a/solution.py
+++ b/solution.py
@@ -8,11 +8,12 @@
 from jax.sharding import PartitionSpec as P
 
 NZ = 16
+FIRST_TILES = 4
 RELAY_HOP = 7
 RELAY_GAP = 5
-COLLECT_HOP = 4
-COLLECT_GAP = 5
-FINISH_HOP = 4
+COLLECT_HOP = 5
+COLLECT_GAP = 7
+FINISH_HOP = 3
 MESH = pl.DeviceIdType.MESH
 F32 = jnp.float32
 BF16 = jnp.bfloat16
@@ -56,9 +57,10 @@
     quart_m = rows_m // 4
     n_in = ny * 16
     n_out = nx * 32
-    first = (width // 128 + 1) // 2 * 128
+    first = min(FIRST_TILES, width // 128 - 1) * 128
     chunks = (pl.ds(0, first), pl.ds(first, width - first))
     both_chunks = range(2)
+    outward_order = (1, 0)
 
     def dev(yy, xx, zz, cc):
         return (yy, xx * NZ + zz, cc)
@@ -161,7 +163,7 @@
 
     for d in range(1, ny):
         send(gather_info(d, (y + d) % ny, y))
-    for n in both_chunks:
+    for n in outward_order:
         for d in range(1, ny):
             send(gather_rows(d, n, (y + d) % ny, y))
 
@@ -217,7 +219,7 @@
             packed.at[to, :, chunks[n]], xbuf.at[src, :, chunks[n]], xs.at[n, d], xr.at[n, d], dev(y, to, z, c)
         )
 
-    for n in both_chunks:
+    for n in outward_order:
         for d in range(1, ny):
             src = (y + ny - d) % ny
             gather_rows(d, n, src, src).wait_recv()
@@ -250,7 +252,7 @@
             dev(y, x, where, c),
         )
 
-    for n in both_chunks:
+    for n in outward_order:
         for d in range(1, nx):
             src = (x + nx - d) % nx
             x_out(d, n, src, src).wait_recv()
@@ -272,8 +274,8 @@
         across(own, n, c).start()
 
     def relay(t, carry):
-        for n in both_chunks:
-            u = t - n * RELAY_GAP
+        for n in outward_order:
+            u = t - (1 - n) * RELAY_GAP
             for rank, step, ends, onward in ((r, -1, r < 3, to_right), (3 - r, 1, r > 0, to_left)):
                 near = (u >= 1) & (u <= RELAY_HOP * rank) & (u % RELAY_HOP == 0)
                 late = u - RELAY_HOP * (rank + 1)
@@ -299,14 +301,14 @@
             across(i, n, other).wait_recv()
         return carry
 
-    lax.fori_loop(0, 16, other_half, 0)
-
     gate = up = back = None
-    for cc in range(2):
+    for half in (c, other):
+        if half is other:
+            lax.fori_loop(0, 16, other_half, 0)
         for h in range(2):
-            rows = zbuf[cc, :, h * half_m:(h + 1) * half_m, :].reshape(16 * half_m, width)
-            k0 = (2 * cc + h) * width
-            parts = [dot(rows, w[k0:k0 + width, :]) for w in (wg, wu, wdt)]
+            rows = zbuf[half, :, h * half_m:(h + 1) * half_m, :].reshape(16 * half_m, width)
+            at = pl.ds(pl.multiple_of(half * (2 * width) + h * width, 128), width)
+            parts = [dot(rows, w[at, :]) for w in (wg, wu, wdt)]
             if gate is None:
                 gate, up, back = parts
             else:
@@ -327,19 +329,22 @@
             obuf.at[other, :, :, chunks[n]], pin.at[:, :, chunks[n]], ps.at[n], pr.at[n], dev(y, x, z, other)
         )
 
-    for n in both_chunks:
+    def produce(half, n):
         size = chunks[n].size
-        for half in (other, c):
-            for h in range(2):
-                at = pl.ds(pl.multiple_of(half * (2 * width) + h * width + chunks[n].start, 128), size)
-                part_out = dot(hidden, wd[:, at])
-                part_in = dot(gate_back, wgt[:, at]) + dot(up_back, wut[:, at])
-                both = jnp.stack(
-                    [part_out.reshape(16, quart_m, size), part_in.reshape(16, quart_m, size)], axis=1
-                ).reshape(16, half_m, size)
-                obuf[half, :, h * half_m:(h + 1) * half_m, chunks[n]] = both.astype(BF16)
-            if half is other:
-                send(partner_sum(n))
+        for h in range(2):
+            at = pl.ds(pl.multiple_of(half * (2 * width) + h * width + chunks[n].start, 128), size)
+            part_out = dot(hidden, wd[:, at])
+            part_in = dot(gate_back, wgt[:, at]) + dot(up_back, wut[:, at])
+            both = jnp.stack(
+                [part_out.reshape(16, quart_m, size), part_in.reshape(16, quart_m, size)], axis=1
+            ).reshape(16, half_m, size)
+            obuf[half, :, h * half_m:(h + 1) * half_m, chunks[n]] = both.astype(BF16)
+
+    produce(other, 0)
+    send(partner_sum(0))
+    produce(c, 0)
+    produce(other, 1)
+    send(partner_sum(1))
 
     def mine(i, n):
         return obuf[c, i, :, chunks[n]].astype(F32) + pin[i, :, chunks[n]].astype(F32)
@@ -442,10 +447,12 @@
         return dot_nt(packed[:, :, chunks[n]].reshape(n_out, chunks[n].size), rows)
 
     partner_sum(0).wait_recv()
-    partner_sum(1).wait_recv()
     first_done = 9 + 3 * COLLECT_HOP + FINISH_HOP
     last = COLLECT_GAP + 9 + 3 * COLLECT_HOP
-    lax.fori_loop(0, first_done, collect, 0)
+    lax.fori_loop(0, COLLECT_GAP, collect, 0)
+    produce(c, 1)
+    partner_sum(1).wait_recv()
+    lax.fori_loop(COLLECT_GAP, first_done, collect, 0)
     finish_z(0)
     lax.fori_loop(first_done, first_done + FINISH_HOP, collect, 0)
     products = finish_x(0)

time: 107 us -> 106 us (level)
  no operation moved by 1% of the time
where the time goes in v3:
time: 106 us
  Pallas kernels  102 us (96%)
  local copies, waits for them, and re-layouts  2.57 us (2%)
    pallas_call x1, Pallas kernels, body(): pl.pallas_call(functools.partial(kernel, ny, nx, 4 * nx), out_shape=(jax....  102 us
    unnamed x7, local copies, waits for them, and re-layouts  2.57 us

profile of v3, /device:TPU:1, one launch (start us, length us, event | category | flops | bytes accessed | tf_op | source)
XLA Modules:
  0.0 105.5 jit_solution(2985356472863919444)
XLA Ops:
  0.6 102.3 %shard_map.103 = (bf16[4,1792]{1,0:T(4,128)(2,1)}, bf16[4,1792]{1,0:T(4,128)(2,1)}, f32[4,4]{1,0:T(4,128)}) custom-call(bf16[4,3584]{1,0:T(4,128)(2,1)} %tok_hbm.1, bf16[4,3584]{1,0:T(4,128)(2,1)} %cot_hbm.1, s32[4,4]{1,0:T(4,128)} %gid_hbm.1, s32[4,8]{1,0:T(4,128)} %eid_hbm.1, bf16[4,8]{1,0:T(4,128)(2,1)} %gw_hbm.1, bf16[1,3584,128]{2,1,0:T(8,128)(2,1)} %wg_hbm.1, ...), custom_call_target="tpu_custom_call" | custom-call | tf_op jit(solution)/shard_map/pallas_call | solution.py:583
  102.9 0.0 copy-start
  103.0 1.3 %copy.14 = bf16[4,1792]{1,0:T(4,128)(2,1)} copy(bf16[4,1792]{1,0:T(4,128)(2,1)} %get-tuple-element.6) | data formatting | bytes 28672
  104.3 0.0 copy-done
  104.3 0.0 copy-start.1
  104.3 0.6 copy.15
  104.9 0.1 copy-done.1
  105.0 0.6 copy.16
Async XLA Ops:
  102.9 1.3 %copy-start = (bf16[4,1792]{1,0:T(4,128)(2,1)S(1)}, bf16[4,1792]{1,0:T(4,128)(2,1)}, u32[]{:S(2)}) copy-start(bf16[4,1792]{1,0:T(4,128)(2,1)} %get-tuple-element.7) | copy-start | bytes 43012
  104.3 0.7 copy-start.1

commit v4 on v3

--- a/solution.py
+++ b/solution.py
@@ -9,11 +9,11 @@
 
 NZ = 16
 FIRST_TILES = 4
-RELAY_HOP = 7
-RELAY_GAP = 5
-COLLECT_HOP = 5
+RELAY_HOP = 8
+RELAY_GAP = 7
+COLLECT_HOP = 4
 COLLECT_GAP = 7
-FINISH_HOP = 3
+FINISH_HOP = 2
 MESH = pl.DeviceIdType.MESH
 F32 = jnp.float32
 BF16 = jnp.bfloat16
@@ -34,8 +34,8 @@
 def kernel(
     ny, nx, per_group,
     tok_hbm, cot_hbm, gid_hbm, eid_hbm, gw_hbm, wg_hbm, wu_hbm, wd_hbm,
-    mixed_hbm, grad_hbm, score_hbm,
-    tok_ref, cot_ref, gid_ref, eid_ref, gw_ref, mixed_ref, grad_ref, score_ref,
+    rows_hbm, score_hbm,
+    tok_ref, cot_ref, gid_ref, eid_ref, gw_ref, rows_ref, score_ref,
     wg, wu, wd, wdt, wgt, wut,
     msg32, gbuf, ibuf, packed, xbuf, mbuf, zbuf, obuf, pin, cbuf, in_left, in_right,
     fin, rp, ret, ymsg, ybuf, smsg, sbuf, half_score, whole_score,
@@ -343,8 +343,6 @@
     produce(other, 0)
     send(partner_sum(0))
     produce(c, 0)
-    produce(other, 1)
-    send(partner_sum(1))
 
     def mine(i, n):
         return obuf[c, i, :, chunks[n]].astype(F32) + pin[i, :, chunks[n]].astype(F32)
@@ -449,10 +447,12 @@
     partner_sum(0).wait_recv()
     first_done = 9 + 3 * COLLECT_HOP + FINISH_HOP
     last = COLLECT_GAP + 9 + 3 * COLLECT_HOP
-    lax.fori_loop(0, COLLECT_GAP, collect, 0)
+    lax.fori_loop(0, COLLECT_HOP, collect, 0)
+    produce(other, 1)
+    send(partner_sum(1))
     produce(c, 1)
     partner_sum(1).wait_recv()
-    lax.fori_loop(COLLECT_GAP, first_done, collect, 0)
+    lax.fori_loop(COLLECT_HOP, first_done, collect, 0)
     finish_z(0)
     lax.fori_loop(first_done, first_done + FINISH_HOP, collect, 0)
     products = finish_x(0)
@@ -492,19 +492,18 @@
     for n in range(ny):
         total = total + ybuf[n].astype(F32)
     for h in range(2):
-        mixed_ref[:, h * width:(h + 1) * width] = total[h * 8:h * 8 + 4].astype(BF16)
-        grad_ref[:, h * width:(h + 1) * width] = total[h * 8 + 4:h * 8 + 8].astype(BF16)
+        rows_ref[:, h * width:(h + 1) * width] = total[h * 8:h * 8 + 4].astype(BF16)
+        rows_ref[:, (2 + h) * width:(3 + h) * width] = total[h * 8 + 4:h * 8 + 8].astype(BF16)
     to_partner.wait_recv()
     score = (half_score[...] + whole_score[...])[0:4]
     outputs = [
         pltpu.make_async_copy(src, dst, osem.at[k])
-        for k, (src, dst) in enumerate(((mixed_ref, mixed_hbm), (grad_ref, grad_hbm), (score_ref, score_hbm)))
+        for k, (src, dst) in enumerate(((rows_ref, rows_hbm), (score_ref, score_hbm)))
     ]
     outputs[0].start()
-    outputs[1].start()
     share = top_k // 2
     score_ref[...] = jnp.where(c == 0, score[:, 0:share], score[:, share:2 * share])
-    outputs[2].start()
+    outputs[1].start()
 
     for cp in sends:
         cp.wait_send()
@@ -560,7 +559,7 @@
         pltpu.VMEM(tokens.shape, BF16), pltpu.VMEM(cotangent.shape, BF16),
         pltpu.VMEM(group_ids.shape, jnp.int32), pltpu.VMEM(expert_ids.shape, jnp.int32),
         pltpu.VMEM(gate_weights.shape, BF16),
-        pltpu.VMEM((n_tok, depth // 2), BF16), pltpu.VMEM((n_tok, depth // 2), BF16),
+        pltpu.VMEM((n_tok, depth), BF16),
         pltpu.VMEM((n_tok, n_pick // 2), F32),
     ]
     scratch = small + [
@@ -574,26 +573,26 @@
         buf(ny, 16, width), buf(ny, 16, width),
         pltpu.VMEM((ny, 8, 128), F32), pltpu.VMEM((ny, 8, 128), F32),
         pltpu.VMEM((8, 128), F32), pltpu.VMEM((8, 128), F32),
-        dma((5,)), dma((3,)), dma((3,)), dma((2, ny)), dma((2, ny)), dma((ny,)), dma((ny,)),
+        dma((5,)), dma((2,)), dma((3,)), dma((2, ny)), dma((2, ny)), dma((ny,)), dma((ny,)),
         dma((2, nx)), dma((2, nx)), dma((2, 3)), dma((2, 16)), dma((2, 16)), dma((2, 16)), dma((2, 16)), dma((2, 16)),
         dma((2,)), dma((2,)),
         dma((2, 10)), dma((2, 10)), dma((2, 10)), dma((2, 10)), dma((2, 16)), dma((2, 4)),
         dma((2, nx)), dma((2, nx)), dma((2, ny)), dma((2, ny)), dma((ny,)), dma((ny,)), dma((1,)), dma((1,)),
     ]
-    return pl.pallas_call(
+    rows, scores = pl.pallas_call(
         functools.partial(kernel, ny, nx, 4 * nx),
         out_shape=(
-            jax.ShapeDtypeStruct((tokens.shape[0], depth // 2), BF16),
-            jax.ShapeDtypeStruct((tokens.shape[0], depth // 2), BF16),
+            jax.ShapeDtypeStruct((tokens.shape[0], depth), BF16),
             jax.ShapeDtypeStruct((tokens.shape[0], expert_ids.shape[1] // 2), F32),
         ),
         in_specs=[hbm] * 8,
-        out_specs=(hbm, hbm, hbm),
+        out_specs=(hbm, hbm),
         scratch_shapes=scratch,
         compiler_params=pltpu.CompilerParams(
             collective_id=0, has_side_effects=True, vmem_limit_bytes=60 * 1024 * 1024
         ),
     )(tokens, cotangent, group_ids, expert_ids, gate_weights, w_gate, w_up, w_down)
+    return rows[:, :depth // 2], rows[:, depth // 2:], scores
 
 
 def solution(mesh):

time: 106 us -> 105 us (level)
    slice x0 -> x1, local copies, waits for them, and re-layouts: none -> 1.34 us  [body(): return (rows[:, :depth // 2], rows[:, depth // 2:], scores)]
    unnamed x7 -> x3, local copies, waits for them, and re-layouts: 2.57 us -> 1.24 us
where the time goes in v4:
time: 105 us
  Pallas kernels  101 us (96%)
  local copies, waits for them, and re-layouts  2.59 us (2%)
    pallas_call x1, Pallas kernels, body(): pl.pallas_call(functools.partial(kernel, ny, nx, 4 * nx), out_shape=(jax....  101 us

profile of v4, /device:TPU:1, one launch (start us, length us, event | category | flops | bytes accessed | tf_op | source)
XLA Modules:
  0.0 104.7 jit_solution(1975371674935433079)
XLA Ops:
  0.6 101.5 %shard_map.103 = (bf16[4,3584]{1,0:T(4,128)(2,1)}, f32[4,4]{1,0:T(4,128)}) custom-call(bf16[4,3584]{1,0:T(4,128)(2,1)} %tok_hbm.1, bf16[4,3584]{1,0:T(4,128)(2,1)} %cot_hbm.1, s32[4,4]{1,0:T(4,128)} %gid_hbm.1, s32[4,8]{1,0:T(4,128)} %eid_hbm.1, bf16[4,8]{1,0:T(4,128)(2,1)} %gw_hbm.1, bf16[1,3584,128]{2,1,0:T(8,128)(2,1)} %wg_hbm.1, ...), custom_call_target="tpu_custom_call" | custom-call | tf_op jit(solution)/shard_map/pallas_call | solution.py:582
  102.1 1.3 %fusion = (bf16[4,1792]{1,0:T(4,128)(2,1)}, bf16[4,1792]{1,0:T(4,128)(2,1)}) fusion(bf16[4,3584]{1,0:T(4,128)(2,1)} %get-tuple-element.5), kind=kLoop, calls=%fused_computation | loop fusion | bytes 57344 | tf_op jit(solution)/shard_map/slice | solution.py:595
  103.5 0.0 copy-start
  103.5 0.7 copy-done
  104.1 0.6 copy.12
Async XLA Ops:
  103.5 0.7 copy-start
